TPU v7x, 32 devices: a whole 2x2x4 slice. The times are simulated.
32 devices in a mesh: row: 4 (over z), col: 4 (over x, core), dep: 2 (over y).
Axes of the slice: x: 2, y: 2, z: 4, core: 2. Of those that a mesh axis runs over, the one named last changes fastest.
Arguments:
- tokens: bfloat16 [512, 8192], P(('dep', 'col'), 'row'), may hold values from -6 to 6
- gate_weight: bfloat16 [8192, 14336], P('row', 'col'), may hold values from -0.0625 to 0.0625
- up_weight: bfloat16 [8192, 14336], P('row', 'col'), may hold values from -0.0625 to 0.0625
- cotangent: bfloat16 [512, 14336], P(('dep', 'row'), 'col'), may hold values from -6 to 6
Outputs:
- hidden: bfloat16 [512, 14336], P(('dep', 'row'), 'col')
- grad_tokens: bfloat16 [512, 8192], P(('dep', 'col'), 'row')
- grad_gate_weight: bfloat16 [8192, 14336], P('row', ('col', 'dep'))
- grad_up_weight: bfloat16 [8192, 14336], P('row', ('col', 'dep'))
All inputs are finite; a program needn't handle non-finite values.
Results may differ from a plain program's by a relative error of at most 0.02.
Values may be sent and summed in bfloat16 or wider, within the bound.
A program may use at most 128 MiB of HBM per device.

v0:
```python
import jax
import jax.numpy as jnp
from jax import lax
from jax.sharding import PartitionSpec as P


def on_device(tokens, gate_weight, up_weight, cotangent):
    width = gate_weight.shape[1]
    gathered = lax.all_gather(tokens, "col", axis=0, tiled=True)
    first = jnp.dot(gathered, gate_weight, preferred_element_type=jnp.float32)
    second = jnp.dot(gathered, up_weight, preferred_element_type=jnp.float32)
    joined = lax.psum_scatter(
        jnp.concatenate([first, second], axis=1).astype(jnp.bfloat16),
        "row",
        scatter_dimension=0,
        tiled=True,
    ).astype(jnp.float32)
    gate = joined[:, :width]
    up = joined[:, width:]
    sigma = jax.nn.sigmoid(gate)
    active = gate * sigma
    hidden = (active * up).astype(jnp.bfloat16)
    upstream = cotangent.astype(jnp.float32)
    grad_gate = (upstream * up * sigma * (1.0 + gate * (1.0 - sigma))).astype(jnp.bfloat16)
    grad_up = (upstream * active).astype(jnp.bfloat16)
    full_gate, full_up = (
        lax.all_gather(grad_gate, "row", axis=0, tiled=True),
        lax.all_gather(grad_up, "row", axis=0, tiled=True),
    )
    transposed = (((1,), (1,)), ((), ()))
    term = lax.dot_general(full_gate, gate_weight, transposed, preferred_element_type=jnp.float32)
    grad_tokens = lax.psum_scatter(
        (
            term
            + lax.dot_general(full_up, up_weight, transposed, preferred_element_type=jnp.float32)
        ).astype(jnp.bfloat16),
        "col",
        scatter_dimension=0,
        tiled=True,
    )
    contract = (((0,), (0,)), ((), ()))
    part_gate = lax.dot_general(gathered, full_gate, contract, preferred_element_type=jnp.float32)
    part_up = lax.dot_general(gathered, full_up, contract, preferred_element_type=jnp.float32)
    sum_gate, sum_up = (
        lax.psum_scatter(
            part_gate.astype(jnp.bfloat16), "dep", scatter_dimension=1, tiled=True
        ).astype(jnp.float32),
        lax.psum_scatter(
            part_up.astype(jnp.bfloat16), "dep", scatter_dimension=1, tiled=True
        ).astype(jnp.float32),
    )
    return (hidden, grad_tokens, sum_gate.astype(jnp.bfloat16), sum_up.astype(jnp.bfloat16))


def solution(mesh):
    return jax.shard_map(
        on_device,
        mesh=mesh,
        in_specs=(
            P(("dep", "col"), "row"),
            P("row", "col"),
            P("row", "col"),
            P(("dep", "row"), "col"),
        ),
        out_specs=(
            P(("dep", "row"), "col"),
            P(("dep", "col"), "row"),
            P("row", ("col", "dep")),
            P("row", ("col", "dep")),
        ),
        check_vma=False,
    )
```

profile of v0, /device:TPU:0, one launch (start us, length us, event | category | flops | bytes accessed | tf_op | source)
XLA Modules:
  0.0 577.9 jit_solution(14428525481826399173)
XLA Ops:
  7.2 0.0 all-gather.4.cloned.1.call-start
  7.2 0.7 all-gather.4.cloned.1.call-update
  7.9 0.0 reduce-scatter.5.cloned.1.call-start
  7.9 21.1 %all-gather.4.cloned.1.call-done = bf16[256,2048]{1,0:T(8,128)(2,1)} async-done(((bf16[64,2048]{1,0:T(8,128)(2,1)}), bf16[256,2048]{1,0:T(8,128)(2,1)}) %all-gather.4.cloned.1.call-update) | async-done | bytes 1048592 | tf_op jit(solution)/shard_map/all_gather | solution.py:9
  29.0 0.0 copy-start
  29.0 9.5 %convolution_convert_fusion.2 = bf16[256,3584]{1,0:T(8,128)(2,1)S(1)} fusion(bf16[256,2048]{1,0:T(8,128)(2,1)} %all-gather.4.cloned.1.call-done, bf16[2048,3584]{1,0:T(8,128)(2,1)} %param.6), kind=kOutput, calls=%fused_computation.4 | convolution fusion | flops 3759013888 | bytes 17563648 | tf_op jit(solution)/shard_map/dot_general | solution.py:11
  38.5 0.0 copy-done
  38.5 9.1 %convolution_convert_fusion.3 = bf16[256,3584]{1,0:T(8,128)(2,1)S(1)} fusion(bf16[256,2048]{1,0:T(8,128)(2,1)S(1)} %copy-done, bf16[2048,3584]{1,0:T(8,128)(2,1)} %param.5), kind=kOutput, calls=%fused_computation.5 | convolution fusion | flops 3759013888 | bytes 17563648 | tf_op jit(solution)/shard_map/dot_general | solution.py:10
  47.7 2.3 pad_maximum_fusion
  49.9 0.0 copy-start.2
  49.9 0.0 reduce-scatter.5.cloned.1.call-update
  50.0 0.0 all-gather.8.cloned.1.call-start
  50.0 68.5 %reduce-scatter.5.cloned.1.call-done = bf16[64,7168]{1,0:T(8,128)(2,1)} async-done(((bf16[256,7168]{1,0:T(8,128)(2,1)}), bf16[64,7168]{1,0:T(8,128)(2,1)}) %reduce-scatter.5.cloned.1.call-update) | async-done | bytes 917520 | tf_op jit(solution)/shard_map/reduce_scatter | solution.py:12
  118.5 1.3 convert_element_type.35
  119.8 0.0 copy-done.2
  119.8 1.6 fusion.6
  121.4 0.0 all-gather.8.cloned.1.call-update
  121.4 0.0 all-gather.6.cloned.1.call-start
  121.4 0.5 all-gather.6.cloned.1.call-update
  122.0 0.0 reduce-scatter.11.cloned.1.call-start
  122.0 41.3 %all-gather.8.cloned.1.call-done = bf16[256,3584]{1,0:T(8,128)(2,1)} async-done(((bf16[64,3584]{1,0:T(8,128)(2,1)}), bf16[256,3584]{1,0:T(8,128)(2,1)}) %all-gather.8.cloned.1.call-update) | async-done | bytes 1835024 | tf_op jit(solution)/shard_map/all_gather | solution.py:28
  163.3 9.0 %fusion.1 = bf16[2048,3584]{0,1:T(8,128)(2,1)} fusion(bf16[256,3584]{1,0:T(8,128)(2,1)} %all-gather.8.cloned.1.call-done, bf16[256,2048]{1,0:T(8,128)(2,1)S(1)} %copy-done), kind=kOutput, calls=%fused_computation.3 | convolution fusion | flops 3765436416 | bytes 17563648 | tf_op jit(solution)/shard_map/dot_general | solution.py:43
  172.3 0.0 reduce-scatter.11.cloned.1.call-update
  172.4 0.0 reduce-scatter.9.cloned.1.call-start
  172.4 33.2 %all-gather.6.cloned.1.call-done = bf16[256,3584]{1,0:T(8,128)(2,1)} async-done(((bf16[64,3584]{1,0:T(8,128)(2,1)}), bf16[256,3584]{1,0:T(8,128)(2,1)}) %all-gather.6.cloned.1.call-update) | async-done | bytes 1835024 | tf_op jit(solution)/shard_map/all_gather | solution.py:27
  205.6 9.5 %fusion = bf16[2048,3584]{0,1:T(8,128)(2,1)} fusion(bf16[256,3584]{1,0:T(8,128)(2,1)} %all-gather.6.cloned.1.call-done, bf16[256,2048]{1,0:T(8,128)(2,1)S(1)} %copy-done), kind=kOutput, calls=%fused_computation.2 | convolution fusion | flops 3765436416 | bytes 17563648 | tf_op jit(solution)/shard_map/dot_general | solution.py:42
  215.1 0.0 reduce-scatter.9.cloned.1.call-update
  215.1 0.0 copy-start.1
  215.1 0.2 reduce-scatter.7.cloned.1.call-start
  215.4 11.1 %fusion.8 = f32[256,2048]{1,0:T(8,128)} fusion(bf16[256,3584]{1,0:T(8,128)(2,1)} %all-gather.6.cloned.1.call-done, bf16[2048,3584]{1,0:T(8,128)(2,1)} %param.5), kind=kOutput, calls=%fused_computation.18 | convolution fusion | flops 3758096384 | bytes 18612224 | tf_op jit(solution)/shard_map/dot_general | solution.py:31
  226.5 0.0 copy-done.1
  226.5 15.9 %fusion.2 = bf16[256,2048]{1,0:T(8,128)(2,1)} fusion(f32[256,2048]{1,0:T(8,128)} %fusion.8, bf16[256,3584]{1,0:T(8,128)(2,1)S(1)} %copy-done.1, bf16[2048,3584]{1,0:T(8,128)(2,1)} %param.6), kind=kOutput, calls=%fused_computation.8 | convolution fusion | flops 3759144960 | bytes 19660800 | tf_op jit(solution)/shard_map/dot_general | solution.py:35
  242.4 0.0 reduce-scatter.7.cloned.1.call-update
  242.5 131.3 %reduce-scatter.11.cloned.1.call-done = bf16[2048,1792]{0,1:T(8,128)(2,1)} async-done(((bf16[2048,3584]{0,1:T(8,128)(2,1)}), bf16[2048,1792]{0,1:T(8,128)(2,1)}) %reduce-scatter.11.cloned.1.call-update) | async-done | bytes 7340048 | tf_op jit(solution)/shard_map/reduce_scatter | solution.py:48
  373.8 10.1 %copy.9 = bf16[2048,1792]{1,0:T(8,128)(2,1)} copy(bf16[2048,1792]{0,1:T(8,128)(2,1)} %reduce-scatter.11.cloned.1.call-done) | data formatting | bytes 14680064
  383.9 159.1 %reduce-scatter.9.cloned.1.call-done = bf16[2048,1792]{0,1:T(8,128)(2,1)} async-done(((bf16[2048,3584]{0,1:T(8,128)(2,1)}), bf16[2048,1792]{0,1:T(8,128)(2,1)}) %reduce-scatter.9.cloned.1.call-update) | async-done | bytes 7340048 | tf_op jit(solution)/shard_map/reduce_scatter | solution.py:45
  543.0 10.0 %copy.8 = bf16[2048,1792]{1,0:T(8,128)(2,1)} copy(bf16[2048,1792]{0,1:T(8,128)(2,1)} %reduce-scatter.9.cloned.1.call-done) | data formatting | bytes 14680064
  553.0 18.1 %reduce-scatter.7.cloned.1.call-done = bf16[64,2048]{1,0:T(8,128)(2,1)} async-done(((bf16[256,2048]{1,0:T(8,128)(2,1)}), bf16[64,2048]{1,0:T(8,128)(2,1)}) %reduce-scatter.7.cloned.1.call-update) | async-done | bytes 262160 | tf_op jit(solution)/shard_map/reduce_scatter | solution.py:32
Async XLA Ops:
  7.2 21.8 %all-gather.4.cloned.1.call-start = ((), (), s32[]{:S(2)}) async-start(), calls=%async_computation.4 | async-start | bytes 1310720 | tf_op jit(solution)/shard_map/all_gather | solution.py:9
  7.9 110.6 %reduce-scatter.5.cloned.1.call-start = ((), (), s32[]{:S(2)}) async-start(), calls=%async_computation.5 | async-start | bytes 4587520 | tf_op jit(solution)/shard_map/reduce_scatter | solution.py:12
  29.0 9.5 %copy-start = (bf16[256,2048]{1,0:T(8,128)(2,1)S(1)}, bf16[256,2048]{1,0:T(8,128)(2,1)}, u32[]{:S(2)}) copy-start(bf16[256,2048]{1,0:T(8,128)(2,1)} %all-gather.4.cloned.1.call-done) | copy-start | bytes 3145732
  49.9 69.9 %copy-start.2 = (bf16[64,3584]{1,0:T(8,128)(2,1)S(1)}, bf16[64,3584]{1,0:T(8,128)(2,1)}, u32[]{:S(2)}) copy-start(bf16[64,3584]{1,0:T(8,128)(2,1)} %param.7) | copy-start | bytes 1376260
  50.0 113.4 %all-gather.8.cloned.1.call-start = ((), (), s32[]{:S(2)}) async-start(), calls=%async_computation.7 | async-start | bytes 2293760 | tf_op jit(solution)/shard_map/all_gather | solution.py:28
  121.4 84.2 %all-gather.6.cloned.1.call-start = ((), (), s32[]{:S(2)}) async-start(), calls=%async_computation.6 | async-start | bytes 2293760 | tf_op jit(solution)/shard_map/all_gather | solution.py:27
  122.0 251.8 %reduce-scatter.11.cloned.1.call-start = ((), (), s32[]{:S(2)}) async-start(), calls=%async_computation.10 | async-start | bytes 22020096 | tf_op jit(solution)/shard_map/reduce_scatter | solution.py:48
  172.4 370.7 %reduce-scatter.9.cloned.1.call-start = ((), (), s32[]{:S(2)}) async-start(), calls=%async_computation.9 | async-start | bytes 22020096 | tf_op jit(solution)/shard_map/reduce_scatter | solution.py:45
  215.1 11.4 %copy-start.1 = (bf16[256,3584]{1,0:T(8,128)(2,1)S(1)}, bf16[256,3584]{1,0:T(8,128)(2,1)}, u32[]{:S(2)}) copy-start(bf16[256,3584]{1,0:T(8,128)(2,1)} %all-gather.8.cloned.1.call-done) | copy-start | bytes 5505028
  215.1 356.0 %reduce-scatter.7.cloned.1.call-start = ((), (), s32[]{:S(2)}) async-start(), calls=%async_computation.8 | async-start | bytes 1310720 | tf_op jit(solution)/shard_map/reduce_scatter | solution.py:32
Sparse Core Ops, SparseCore 0:
  9.6 19.4 all-gather.3
  50.1 68.3 reduce-scatter.4
  121.5 41.7 all-gather.7
  165.3 40.2 all-gather.5
  207.8 165.9 reduce-scatter.10
  375.9 167.0 reduce-scatter.8
  546.1 24.9 reduce-scatter.6
where the time goes:
time: 579 us; the launch traced here: 578 us
  waiting for transfers between devices  474 us (82%)
  matrix products  64.2 us (11%)
  local copies, waits for them, and re-layouts  20.1 us (3%)
  between operations  14.2 us (2%)
    reduce_scatter x1, waiting for transfers between devices, on_device(): lax.psum_scatter(part_gate.astype(jnp.bfloat16), 'dep', scatter_dimension...  159 us
    reduce_scatter x1, waiting for transfers between devices, on_device(): lax.psum_scatter(part_up.astype(jnp.bfloat16), 'dep', scatter_dimension=1...  131 us
    reduce_scatter x1, waiting for transfers between devices, on_device(): lax.psum_scatter(jnp.concatenate([first, second], axis=1).astype(jnp.bflo...  68.5 us
    all_gather x1, waiting for transfers between devices, on_device(): lax.all_gather(grad_up, 'row', axis=0, tiled=True)  41.3 us
    all_gather x1, waiting for transfers between devices, on_device(): lax.all_gather(grad_gate, 'row', axis=0, tiled=True)  33.2 us
    all_gather x1, waiting for transfers between devices, on_device(): gathered = lax.all_gather(tokens, 'col', axis=0, tiled=True)  21.1 us
    unnamed x8, local copies, waits for them, and re-layouts  20.1 us
    reduce_scatter x1, waiting for transfers between devices, on_device(): lax.psum_scatter((term + lax.dot_general(full_up, up_weight, transposed,...  18.1 us
  transfers between devices with their start and end apart: 7, of which 7 were waited for; matrix products, arithmetic and copies ran while one was open for 11% of the time, Pallas kernels for 0%

commit v1 on v0

v1 whole, which is shorter than its diff:
```python
import jax
import jax.numpy as jnp
from jax import lax
from jax.sharding import PartitionSpec as P


def swapped(block, n_dep):
    parts = [block]
    for _ in range(n_dep - 1):
        parts.append(lax.ppermute(parts[-1], "dep", [(i, (i + 1) % n_dep) for i in range(n_dep)]))
    return parts


def on_device(n_dep, tokens, gate_weight, up_weight, cotangent):
    width = gate_weight.shape[1]
    share = width // n_dep
    me = lax.axis_index("dep")
    gathered = lax.all_gather(tokens, "col", axis=0, tiled=True)
    all_tokens = jnp.concatenate(swapped(gathered, n_dep), axis=0)

    def dot(a, b):
        return jnp.dot(a, b, preferred_element_type=jnp.float32)

    def scattered(part):
        return lax.psum_scatter(
            part.astype(jnp.bfloat16), "row", scatter_dimension=0, tiled=True
        ).astype(jnp.float32)

    gate = scattered(dot(gathered, gate_weight))
    up = scattered(dot(gathered, up_weight))
    sigma = jax.nn.sigmoid(gate)
    active = gate * sigma
    hidden = (active * up).astype(jnp.bfloat16)
    upstream = cotangent.astype(jnp.float32)
    grad_gate = (upstream * up * sigma * (1.0 + gate * (1.0 - sigma))).astype(jnp.bfloat16)
    grad_up = (upstream * active).astype(jnp.bfloat16)
    full_up = lax.all_gather(grad_up, "row", axis=0, tiled=True)
    full_gate = lax.all_gather(grad_gate, "row", axis=0, tiled=True)

    def exchanged(full):
        parts = [lax.dynamic_slice_in_dim(full, me * share, share, 1)]
        for step in range(1, n_dep):
            to = lax.rem(me + step, n_dep)
            block = lax.dynamic_slice_in_dim(full, to * share, share, 1)
            parts.append(lax.ppermute(block, "dep", [(i, (i + step) % n_dep) for i in range(n_dep)]))
        return jnp.concatenate(parts, axis=0)

    transposed = (((1,), (1,)), ((), ()))
    contract = (((0,), (0,)), ((), ()))
    all_up = exchanged(full_up)
    all_gate = exchanged(full_gate)
    term = lax.dot_general(full_up, up_weight, transposed, preferred_element_type=jnp.float32)
    term = term + lax.dot_general(full_gate, gate_weight, transposed, preferred_element_type=jnp.float32)
    grad_tokens = lax.psum_scatter(
        term.astype(jnp.bfloat16), "col", scatter_dimension=0, tiled=True
    )
    sum_up = lax.dot_general(all_tokens, all_up, contract, preferred_element_type=jnp.float32)
    sum_gate = lax.dot_general(all_tokens, all_gate, contract, preferred_element_type=jnp.float32)
    return (hidden, grad_tokens, sum_gate.astype(jnp.bfloat16), sum_up.astype(jnp.bfloat16))


def solution(mesh):
    n_dep = mesh.shape["dep"]
    return jax.shard_map(
        lambda *args: on_device(n_dep, *args),
        mesh=mesh,
        in_specs=(
            P(("dep", "col"), "row"),
            P("row", "col"),
            P("row", "col"),
            P(("dep", "row"), "col"),
        ),
        out_specs=(
            P(("dep", "row"), "col"),
            P(("dep", "col"), "row"),
            P("row", ("col", "dep")),
            P("row", ("col", "dep")),
        ),
        check_vma=False,
    )
```

time: 579 us -> 254 us (0.44)
  waiting for transfers between devices: 474 us -> 173 us
  local copies, waits for them, and re-layouts: 20.1 us -> 5.88 us
  matrix products: 64.2 us -> 52.8 us
    reduce_scatter x4 -> x3, waiting for transfers between devices: 377 us -> 70.6 us  [the longest x2 70.6 us: scattered(): lax.psum_scatter(part.astype(jnp.bfloat16), 'row', scatter_dimension=0, t...]
    unnamed x8 -> x11, local copies, waits for them, and re-layouts: 20.1 us -> 1.48 us
    ppermute x0 -> x3, waiting for transfers between devices: none -> 12 us  [the longest x2 12 us: exchanged(): lax.ppermute(block, 'dep', [(i, (i + step) % n_dep) for i in range(n_dep)])]
    dot_general x1, matrix products: 15.9 us -> 7.74 us  [on_device(): lax.dot_general(full_up, up_weight, transposed, preferred_element_type=jn...]
    all_gather x2, waiting for transfers between devices: 74.6 us -> 67.9 us  [the longest x1 38.3 us: on_device(): full_up = lax.all_gather(grad_up, 'row', axis=0, tiled=True)]
  transfers between devices with their start and end apart: 7 -> 9, of which waited for: 7 -> 6; matrix products, arithmetic and copies ran while one was open for 11% -> 18% of each run, Pallas kernels for 0% -> 0%
where the time goes in v1:
time: 254 us; the launch traced here: 253 us
  waiting for transfers between devices  173 us (68%)
  matrix products  52.8 us (21%)
  between operations  14.2 us (6%)
  local copies, waits for them, and re-layouts  5.88 us (2%)
  starting transfers between devices  4.97 us (2%)
  other arithmetic  2.69 us (1%)
    reduce_scatter x2, waiting for transfers between devices, scattered(): lax.psum_scatter(part.astype(jnp.bfloat16), 'row', scatter_dimension=0, t...  70.6 us
    all_gather x1, waiting for transfers between devices, on_device(): full_up = lax.all_gather(grad_up, 'row', axis=0, tiled=True)  38.3 us
    all_gather x1, waiting for transfers between devices, on_device(): full_gate = lax.all_gather(grad_gate, 'row', axis=0, tiled=True)  29.6 us
    all_gather x1, waiting for transfers between devices, on_device(): gathered = lax.all_gather(tokens, 'col', axis=0, tiled=True)  21.1 us
    dot_general x2, matrix products, dot(): return jnp.dot(a, b, preferred_element_type=jnp.float32)  21 us
    ppermute x2, waiting for transfers between devices, exchanged(): lax.ppermute(block, 'dep', [(i, (i + step) % n_dep) for i in range(n_dep)])  12 us
    dot_general x1, matrix products, on_device(): lax.dot_general(full_gate, gate_weight, transposed, preferred_element_typ...  10.7 us
    dot_general x1, matrix products, on_device(): lax.dot_general(full_up, up_weight, transposed, preferred_element_type=jn...  7.74 us
  transfers between devices with their start and end apart: 9, of which 6 were waited for; matrix products, arithmetic and copies ran while one was open for 18% of the time, Pallas kernels for 0%

profile of v1, /device:TPU:0, one launch (start us, length us, event | category | flops | bytes accessed | tf_op | source)
XLA Modules:
  0.0 253.4 jit_solution(15776171901941478018)
XLA Ops:
  7.2 0.0 all-gather.4.cloned.1.call-start
  7.2 0.7 all-gather.4.cloned.1.call-update
  7.9 0.0 reduce-scatter.6.cloned.1.call-start
  7.9 21.1 %all-gather.4.cloned.1.call-done = bf16[256,2048]{1,0:T(8,128)(2,1)} async-done(((bf16[64,2048]{1,0:T(8,128)(2,1)}), bf16[256,2048]{1,0:T(8,128)(2,1)}) %all-gather.4.cloned.1.call-update) | async-done | bytes 1048592 | tf_op jit(solution)/shard_map/all_gather | solution.py:18
  29.0 0.0 copy-start.2
  29.0 10.8 %convolution_convert_fusion.2 = bf16[256,3584]{1,0:T(8,128)(2,1)} fusion(bf16[256,2048]{1,0:T(8,128)(2,1)} %all-gather.4.cloned.1.call-done, bf16[2048,3584]{1,0:T(8,128)(2,1)} %param.6), kind=kOutput, calls=%fused_computation.2 | convolution fusion | flops 3759013888 | bytes 17563648 | tf_op jit(solution)/shard_map/dot_general | solution.py:22
  39.8 0.0 reduce-scatter.6.cloned.1.call-update
  39.8 0.0 reduce-scatter.4.cloned.1.call-start
  39.8 0.0 copy-done.2
  39.9 10.3 %convolution_convert_fusion.3 = bf16[256,3584]{1,0:T(8,128)(2,1)} fusion(bf16[256,2048]{1,0:T(8,128)(2,1)S(1)} %copy-done.2, bf16[2048,3584]{1,0:T(8,128)(2,1)} %param.5), kind=kOutput, calls=%fused_computation.3 | convolution fusion | flops 3759013888 | bytes 17563648 | tf_op jit(solution)/shard_map/dot_general | solution.py:22
  50.1 0.0 copy-start.4
  50.1 0.0 reduce-scatter.4.cloned.1.call-update
  50.2 0.0 all-gather.6.cloned.1.call-start
  50.2 29.2 %reduce-scatter.6.cloned.1.call-done = bf16[64,3584]{1,0:T(8,128)(2,1)} async-done(((bf16[256,3584]{1,0:T(8,128)(2,1)}), bf16[64,3584]{1,0:T(8,128)(2,1)}) %reduce-scatter.6.cloned.1.call-update) | async-done | bytes 458768 | tf_op jit(solution)/shard_map/reduce_scatter | solution.py:25
  79.4 41.5 %reduce-scatter.4.cloned.1.call-done = bf16[64,3584]{1,0:T(8,128)(2,1)} async-done(((bf16[256,3584]{1,0:T(8,128)(2,1)}), bf16[64,3584]{1,0:T(8,128)(2,1)}) %reduce-scatter.4.cloned.1.call-update) | async-done | bytes 458768 | tf_op jit(solution)/shard_map/reduce_scatter | solution.py:25
  120.8 0.0 copy-done.4
  120.8 2.7 %fusion.11 = (bf16[64,3584]{1,0:T(8,128)(2,1)}, bf16[64,3584]{1,0:T(8,128)(2,1)}, bf16[64,3584]{1,0:T(8,128)(2,1)}) fusion(bf16[64,3584]{1,0:T(8,128)(2,1)} %reduce-scatter.6.cloned.1.call-done, bf16[64,3584]{1,0:T(8,128)(2,1)S(1)} %copy-done.4, bf16[64,3584]{1,0:T(8,128)(2,1)} %reduce-scatter.4.cloned.1.call-done), kind=kLoop, calls=%fused_computation.22 | loop fusion | flops 4128768 | bytes 2752512 | tf_op jit(solution)/shard_map/convert_element_type | solution.py:35
  123.5 0.0 all-gather.6.cloned.1.call-update
  123.5 0.0 all-gather.8.cloned.1.call-start
  123.6 0.5 all-gather.8.cloned.1.call-update
  124.1 0.2 reduce-scatter.8.cloned.1.call-start
  124.4 1.5 collective-permute-start
  125.9 38.3 %all-gather.6.cloned.1.call-done = bf16[256,3584]{1,0:T(8,128)(2,1)} async-done(((bf16[64,3584]{1,0:T(8,128)(2,1)}), bf16[256,3584]{1,0:T(8,128)(2,1)}) %all-gather.6.cloned.1.call-update) | async-done | bytes 1835024 | tf_op jit(solution)/shard_map/all_gather | solution.py:37
  164.2 0.0 copy-start.1
  164.2 2.9 %constant_dynamic-slice_fusion.1 = (bf16[256,1792]{1,0:T(8,128)(2,1)}, bf16[256,1792]{1,0:T(8,128)(2,1)}) fusion(bf16[256,3584]{1,0:T(8,128)(2,1)} %all-gather.6.cloned.1.call-done, s32[]{:T(128)S(6)} %select_n.8, s32[]{:T(128)S(6)} %select_n.9), kind=kLoop, calls=%fused_computation.30 | loop fusion | bytes 3670024 | tf_op jit(solution)/shard_map/dynamic_slice | solution.py:41
  167.2 1.5 collective-permute-start.2
  168.6 0.0 copy-done.1
  168.6 7.7 %fusion.18 = f32[256,2048]{1,0:T(8,128)S(1)} fusion(bf16[256,3584]{1,0:T(8,128)(2,1)S(1)} %copy-done.1, bf16[2048,3584]{1,0:T(8,128)(2,1)} %param.6), kind=kOutput, calls=%fused_computation.35 | convolution fusion | flops 3758096384 | bytes 18612224 | tf_op jit(solution)/shard_map/dot_general | solution.py:52
  176.4 29.6 %all-gather.8.cloned.1.call-done = bf16[256,3584]{1,0:T(8,128)(2,1)} async-done(((bf16[64,3584]{1,0:T(8,128)(2,1)}), bf16[256,3584]{1,0:T(8,128)(2,1)}) %all-gather.8.cloned.1.call-update) | async-done | bytes 1835024 | tf_op jit(solution)/shard_map/all_gather | solution.py:38
  206.0 10.7 %fusion = bf16[256,2048]{1,0:T(8,128)(2,1)} fusion(f32[256,2048]{1,0:T(8,128)S(1)} %fusion.18, bf16[256,3584]{1,0:T(8,128)(2,1)} %all-gather.8.cloned.1.call-done, bf16[2048,3584]{1,0:T(8,128)(2,1)} %param.5), kind=kOutput, calls=%fused_computation.5 | convolution fusion | flops 3759144960 | bytes 19660800 | tf_op jit(solution)/shard_map/dot_general | solution.py:53
  216.7 0.0 copy-start
  216.7 0.0 reduce-scatter.8.cloned.1.call-update
  216.7 0.1 constant_dynamic-update-slice_fusion.1
  216.8 1.4 copy-done
  218.2 0.0 copy-start.3
  218.2 0.1 constant_dynamic-slice_fusion.3
  218.3 1.5 collective-permute-start.1
  219.8 0.0 collective-permute-done
  219.8 1.3 constant_dynamic-update-slice_fusion
  221.2 0.0 collective-permute-done.2
  221.2 0.0 copy-done.3
  221.2 7.3 %convolution_convert_fusion = bf16[2048,1792]{1,0:T(8,128)(2,1)} fusion(bf16[512,2048]{1,0:T(8,128)(2,1)S(1)} %constant_dynamic-update-slice_fusion, bf16[256,1792]{1,0:T(8,128)(2,1)} %collective-permute-done.2, bf16[256,1792]{1,0:T(8,128)(2,1)S(1)} %copy-done.3), kind=kOutput, calls=%fused_computation | convolution fusion | flops 3765436416 | bytes 11272192 | tf_op jit(solution)/shard_map/dot_general | solution.py:57
  228.5 11.9 %collective-permute-done.1 = bf16[256,1792]{1,0:T(8,128)(2,1)S(1)} collective-permute-done((bf16[256,1792]{1,0:T(8,128)(2,1)S(1)}, bf16[256,1792]{1,0:T(8,128)(2,1)S(1)}, u32[]{:S(2)}, u32[]{:S(2)}) %collective-permute-start.1) | collective-permute-done | bytes 917536 | tf_op jit(solution)/shard_map/ppermute | solution.py:45
  240.4 6.1 %convolution_convert_fusion.1 = bf16[2048,1792]{1,0:T(8,128)(2,1)} fusion(bf16[512,2048]{1,0:T(8,128)(2,1)S(1)} %constant_dynamic-update-slice_fusion, bf16[256,1792]{1,0:T(8,128)(2,1)S(1)} %collective-permute-done.1, bf16[256,1792]{1,0:T(8,128)(2,1)S(1)} %get-tuple-element.6), kind=kOutput, calls=%fused_computation.1 | convolution fusion | flops 3765436416 | bytes 11272192 | tf_op jit(solution)/shard_map/dot_general | solution.py:58
  246.5 0.0 reduce-scatter.8.cloned.1.call-done
Async XLA Ops:
  7.2 21.8 %all-gather.4.cloned.1.call-start = ((), (), s32[]{:S(2)}) async-start(), calls=%async_computation.3 | async-start | bytes 1310720 | tf_op jit(solution)/shard_map/all_gather | solution.py:18
  7.9 71.5 %reduce-scatter.6.cloned.1.call-start = ((), (), s32[]{:S(2)}) async-start(), calls=%async_computation.5 | async-start | bytes 2293760 | tf_op jit(solution)/shard_map/reduce_scatter | solution.py:25
  29.0 10.8 %copy-start.2 = (bf16[256,2048]{1,0:T(8,128)(2,1)S(1)}, bf16[256,2048]{1,0:T(8,128)(2,1)}, u32[]{:S(2)}) copy-start(bf16[256,2048]{1,0:T(8,128)(2,1)} %all-gather.4.cloned.1.call-done) | copy-start | bytes 3145732
  39.8 81.0 %reduce-scatter.4.cloned.1.call-start = ((), (), s32[]{:S(2)}) async-start(), calls=%async_computation.4 | async-start | bytes 2293760 | tf_op jit(solution)/shard_map/reduce_scatter | solution.py:25
  50.1 70.7 %copy-start.4 = (bf16[64,3584]{1,0:T(8,128)(2,1)S(1)}, bf16[64,3584]{1,0:T(8,128)(2,1)}, u32[]{:S(2)}) copy-start(bf16[64,3584]{1,0:T(8,128)(2,1)} %param.7) | copy-start | bytes 1376260
  50.2 114.1 %all-gather.6.cloned.1.call-start = ((), (), s32[]{:S(2)}) async-start(), calls=%async_computation.6 | async-start | bytes 2293760 | tf_op jit(solution)/shard_map/all_gather | solution.py:37
  123.5 82.4 %all-gather.8.cloned.1.call-start = ((), (), s32[]{:S(2)}) async-start(), calls=%async_computation.7 | async-start | bytes 2293760 | tf_op jit(solution)/shard_map/all_gather | solution.py:38
  124.1 122.4 %reduce-scatter.8.cloned.1.call-start = ((), (), s32[]{:S(2)}) async-start(), calls=%async_computation.8 | async-start | bytes 1310720 | tf_op jit(solution)/shard_map/reduce_scatter | solution.py:54
  124.4 95.4 %collective-permute-start = (bf16[256,2048]{1,0:T(8,128)(2,1)S(1)}, bf16[256,2048]{1,0:T(8,128)(2,1)}, u32[]{:S(2)}, u32[]{:S(2)}) collective-permute-start(bf16[256,2048]{1,0:T(8,128)(2,1)S(1)} %copy-done.2), channel_id=1, source_target_pairs={{0,1},{1,0},{2,3},{3,2},{4,5},{5,4},{6,7},{7,6},{8,9},{9,8},{10,11... | collective-permute-start | bytes 3145736 | tf_op jit(solution)/shard_map/ppermute | solution.py:10
  164.2 4.4 %copy-start.1 = (bf16[256,3584]{1,0:T(8,128)(2,1)S(1)}, bf16[256,3584]{1,0:T(8,128)(2,1)}, u32[]{:S(2)}) copy-start(bf16[256,3584]{1,0:T(8,128)(2,1)} %all-gather.6.cloned.1.call-done) | copy-start | bytes 5505028
  167.2 54.0 %collective-permute-start.2 = (bf16[256,1792]{1,0:T(8,128)(2,1)}, bf16[256,1792]{1,0:T(8,128)(2,1)}, u32[]{:S(2)}, u32[]{:S(2)}) collective-permute-start(bf16[256,1792]{1,0:T(8,128)(2,1)} %get-tuple-element.5), channel_id=1, source_target_pairs={{0,1},{1,0},{2,3},{3,2},{4,5},{5,4},{6,7},{7,6},{8,9},{9,8},{10,11... | collective-permute-start | bytes 2752520 | tf_op jit(solution)/shard_map/ppermute | solution.py:45
  216.7 1.5 copy-start
  218.2 3.0 %copy-start.3 = (bf16[256,1792]{1,0:T(8,128)(2,1)S(1)}, bf16[256,1792]{1,0:T(8,128)(2,1)}, u32[]{:S(2)}) copy-start(bf16[256,1792]{1,0:T(8,128)(2,1)} %get-tuple-element.4) | copy-start | bytes 2752516
  218.3 22.2 %collective-permute-start.1 = (bf16[256,1792]{1,0:T(8,128)(2,1)S(1)}, bf16[256,1792]{1,0:T(8,128)(2,1)S(1)}, u32[]{:S(2)}, u32[]{:S(2)}) collective-permute-start(bf16[256,1792]{1,0:T(8,128)(2,1)S(1)} %get-tuple-element.7), channel_id=1, source_target_pairs={{0,1},{1,0},{2,3},{3,2},{4,5},{5,4},{6,7},{7,6},{8,9},{9,8},{10,11... | collective-permute-start | bytes 2752520 | tf_op jit(solution)/shard_map/ppermute | solution.py:45
Sparse Core Ops, SparseCore 0:
  9.6 19.4 all-gather.3
  39.9 39.4 reduce-scatter.5
  82.2 38.5 reduce-scatter.3
  123.7 40.5 all-gather.5
  165.7 40.2 all-gather.7
  216.8 23.7 reduce-scatter.7

commit v2 on v0

v2 whole, which is shorter than its diff:
```python
import functools

import jax
import jax.numpy as jnp
from jax import lax
from jax.experimental import pallas as pl
from jax.experimental.pallas import tpu as pltpu
from jax.sharding import PartitionSpec as P

MESH = pl.DeviceIdType.MESH
WIDTH = 128


def kernel(
    n_row, n_col, n_dep, w,
    tokens_ref, gate_w_ref, up_w_ref, cot_ref,
    hidden_ref, part_ref, all_tok_ref, all_gate_ref, all_up_ref,
    tok, weights, own, from_left, from_right, grads, acc,
    w_sem, tok_send, tok_recv, tok_local, slice_send, slice_recv,
    rs_send, left_recv, right_recv, ag_right_send, ag_left_send, ag_recv,
    dep_send, dep_recv, dep_local,
):
    me = lax.axis_index("row")
    my_col = lax.axis_index("col")
    my_dep = lax.axis_index("dep")
    chunks = weights.shape[0]
    depth = weights.shape[1]
    lanes = weights.shape[2]
    share = all_gate_ref.shape[3]
    last = n_row - 1
    out_refs = (all_gate_ref, all_up_ref)
    tokens_n = tok.shape[0] * tok.shape[1]

    def weight_copy(c, h, k):
        ref = (gate_w_ref, up_w_ref)[k]
        at = pl.multiple_of(h * share + c * w, w)
        return pltpu.make_async_copy(
            ref.at[:, pl.ds(at, w)],
            weights.at[c, :, pl.ds((h * 2 + k) * w, w)],
            w_sem.at[c, h * 2 + k],
        )

    def load_weights(c):
        for h in range(n_dep):
            for k in range(2):
                weight_copy(c, h, k).start()

    @pl.loop(0, chunks)
    def _(c):
        load_weights(c)

    barrier = pltpu.get_barrier_semaphore()
    for step in range(1, n_col):
        pl.semaphore_signal(barrier, inc=1, device_id={"col": lax.rem(my_col + step, n_col)}, device_id_type=MESH)
    for step in range(1, n_dep):
        pl.semaphore_signal(barrier, inc=1, device_id={"dep": lax.rem(my_dep + step, n_dep)}, device_id_type=MESH)

    @pl.when(me > 0)
    def _():
        pl.semaphore_signal(barrier, inc=1, device_id={"row": me - 1}, device_id_type=MESH)

    @pl.when(me < last)
    def _():
        pl.semaphore_signal(barrier, inc=1, device_id={"row": me + 1}, device_id_type=MESH)

    peers = n_col - 1 + n_dep - 1
    inside = jnp.logical_and(me > 0, me < last)

    @pl.when(inside)
    def _():
        pl.semaphore_wait(barrier, peers + 2)

    @pl.when(jnp.logical_not(inside))
    def _():
        pl.semaphore_wait(barrier, peers + 1)

    def token_copy(step):
        return pltpu.make_async_remote_copy(
            src_ref=tokens_ref, dst_ref=tok.at[my_col],
            send_sem=tok_send.at[step], recv_sem=tok_recv.at[step],
            device_id={"col": lax.rem(my_col + step, n_col)}, device_id_type=MESH,
        )

    for step in range(1, n_col):
        token_copy(step).start()
    tok[pl.ds(my_col, 1)] = tokens_ref[...][None]
    acc[...] = jnp.zeros_like(acc)
    for step in range(1, n_col):
        token_copy(step).wait_recv()

    def slice_copy(step):
        return pltpu.make_async_remote_copy(
            src_ref=tok, dst_ref=all_tok_ref.at[my_dep],
            send_sem=slice_send.at[step], recv_sem=slice_recv.at[step],
            device_id={"dep": lax.rem(my_dep + step, n_dep)}, device_id_type=MESH,
        )

    tok_out = pltpu.make_async_copy(tok, all_tok_ref.at[my_dep], tok_local)
    for step in range(1, n_dep):
        slice_copy(step).start()
    tok_out.start()

    def rs_right(c, j):
        return pltpu.make_async_remote_copy(
            src_ref=own.at[c, j], dst_ref=from_left.at[c, j],
            send_sem=rs_send.at[c, j], recv_sem=left_recv.at[c, j],
            device_id={"row": me + 1}, device_id_type=MESH,
        )

    def rs_left(c, j):
        return pltpu.make_async_remote_copy(
            src_ref=own.at[c, j], dst_ref=from_right.at[c, j],
            send_sem=rs_send.at[c, j], recv_sem=right_recv.at[c, j],
            device_id={"row": me - 1}, device_id_type=MESH,
        )

    def ag_right(c, j):
        return pltpu.make_async_remote_copy(
            src_ref=grads.at[c, j], dst_ref=grads.at[c, j],
            send_sem=ag_right_send.at[c, j], recv_sem=ag_recv.at[c, j],
            device_id={"row": me + 1}, device_id_type=MESH,
        )

    def ag_left(c, j):
        return pltpu.make_async_remote_copy(
            src_ref=grads.at[c, j], dst_ref=grads.at[c, j],
            send_sem=ag_left_send.at[c, j], recv_sem=ag_recv.at[c, j],
            device_id={"row": me - 1}, device_id_type=MESH,
        )

    def dep_copy(c, step, k):
        to = lax.rem(my_dep + step, n_dep)
        return pltpu.make_async_remote_copy(
            src_ref=grads.at[c, :, :, pl.ds(pl.multiple_of((to * 2 + k) * w, w), w)],
            dst_ref=out_refs[k].at[my_dep, :, :, pl.ds(pl.multiple_of(c * w, w), w)],
            send_sem=dep_send.at[c, step, k], recv_sem=dep_recv.at[c, step, k],
            device_id={"dep": to}, device_id_type=MESH,
        )

    def dep_own(c, k):
        return pltpu.make_async_copy(
            grads.at[c, :, :, pl.ds(pl.multiple_of((my_dep * 2 + k) * w, w), w)],
            out_refs[k].at[my_dep, :, :, pl.ds(pl.multiple_of(c * w, w), w)],
            dep_local.at[c, k],
        )

    def valid(c):
        return jnp.logical_and(c >= 0, c < chunks)

    def forward(c):
        for h in range(n_dep):
            for k in range(2):
                weight_copy(c, h, k).wait()
        lhs = tok[...].reshape(tokens_n, depth)
        for at in range(0, lanes, 256):
            own[c, :, :, at:at + 256] = (
                jnp.dot(lhs, weights[c, :, at:at + 256], preferred_element_type=jnp.float32)
                .astype(jnp.bfloat16)
                .reshape(n_row, tokens_n // n_row, 256)
            )

    def added(ref, other):
        ref[...] = (ref[...].astype(jnp.float32) + other[...].astype(jnp.float32)).astype(jnp.bfloat16)

    def reduce_right(c):
        for j in range(1, n_row):
            @pl.when(j > me)
            def _():
                @pl.when(me > 0)
                def _():
                    rs_right(c, j).wait_recv()
                    added(own.at[c, j], from_left.at[c, j])
                rs_right(c, j).start()

    def reduce_left(c):
        for j in range(n_row - 1):
            @pl.when(j < me)
            def _():
                @pl.when(me < last)
                def _():
                    rs_left(c, j).wait_recv()
                    added(own.at[c, j], from_right.at[c, j])
                rs_left(c, j).start()

    def finish(c):
        @pl.when(me > 0)
        def _():
            rs_right(c, me).wait_recv()

        @pl.when(me < last)
        def _():
            rs_left(c, me).wait_recv()

        for h in range(n_dep):
            at = h * 2 * w

            def total(lo):
                piece = pl.ds(lo, w)
                value = own[c, me, :, piece].astype(jnp.float32)
                value = value + jnp.where(me > 0, from_left[c, me, :, piece].astype(jnp.float32), 0.0)
                return value + jnp.where(me < last, from_right[c, me, :, piece].astype(jnp.float32), 0.0)

            gate, up = total(at), total(at + w)
            sigma = 1.0 / (1.0 + jnp.exp(-gate))
            active = gate * sigma
            columns = pl.ds(pl.multiple_of(h * share + c * w, w), w)
            hidden_ref[:, columns] = (active * up).astype(jnp.bfloat16)
            upstream = cot_ref[:, columns].astype(jnp.float32)
            grads[c, me, :, pl.ds(at, w)] = (
                upstream * up * sigma * (1.0 + gate * (1.0 - sigma))
            ).astype(jnp.bfloat16)
            grads[c, me, :, pl.ds(at + w, w)] = (upstream * active).astype(jnp.bfloat16)

        @pl.when(me < last)
        def _():
            ag_right(c, me).start()

        @pl.when(me > 0)
        def _():
            ag_left(c, me).start()

    def relay(t):
        for away in range(1, n_row):
            c = t - last - away

            @pl.when(valid(c))
            def _():
                @pl.when(me - away >= 0)
                def _():
                    ag_right(c, me - away).wait_recv()

                    @pl.when(me < last)
                    def _():
                        ag_right(c, me - away).start()

                @pl.when(me + away <= last)
                def _():
                    ag_left(c, me + away).wait_recv()

                    @pl.when(me > 0)
                    def _():
                        ag_left(c, me + away).start()

    def backward(c):
        for step in range(1, n_dep):
            for k in range(2):
                dep_copy(c, step, k).start()
        for k in range(2):
            dep_own(c, k).start()
        lhs = grads[c].reshape(tokens_n, lanes)
        tile = min(512, depth)

        @pl.loop(0, depth // tile)
        def _(i):
            rows = pl.ds(pl.multiple_of(i * tile, tile), tile)
            acc[:, rows] += lax.dot_general(
                lhs, weights[c, rows, :], (((1,), (1,)), ((), ())), preferred_element_type=jnp.float32
            )

    @pl.loop(0, chunks + 2 * last)
    def _(t):
        @pl.when(t < chunks)
        def _():
            forward(t)

        c_right = t - me
        @pl.when(valid(c_right))
        def _():
            reduce_right(c_right)

        c_left = t - (last - me)
        @pl.when(valid(c_left))
        def _():
            reduce_left(c_left)

        relay(t)

        c_own = t - last
        @pl.when(valid(c_own))
        def _():
            finish(c_own)

        c_back = t - last - jnp.maximum(me, last - me)
        @pl.when(valid(c_back))
        def _():
            backward(c_back)

    part_ref[...] = acc[...].astype(jnp.bfloat16)

    for step in range(1, n_col):
        token_copy(step).wait_send()
    for step in range(1, n_dep):
        slice_copy(step).wait()
    tok_out.wait()

    @pl.loop(0, chunks)
    def _(c):
        for j in range(n_row):
            @pl.when(j > me)
            def _():
                rs_right(c, j).wait_send()

            @pl.when(j < me)
            def _():
                rs_left(c, j).wait_send()

            @pl.when(jnp.logical_and(j <= me, me < last))
            def _():
                ag_right(c, j).wait_send()

            @pl.when(jnp.logical_and(j >= me, me > 0))
            def _():
                ag_left(c, j).wait_send()
        for k in range(2):
            for step in range(1, n_dep):
                dep_copy(c, step, k).wait()
            dep_own(c, k).wait()


def exchange(n_row, n_col, n_dep, tokens, gate_weight, up_weight, cotangent):
    rows, depth = tokens.shape
    width = gate_weight.shape[1]
    share = width // n_dep
    w = WIDTH
    chunks = share // w
    lanes = 2 * n_dep * w
    tokens_n = rows * n_col
    block = tokens_n // n_row
    bf16 = jnp.bfloat16
    vmem, hbm = pl.BlockSpec(memory_space=pltpu.VMEM), pl.BlockSpec(memory_space=pl.ANY)
    dma = pltpu.SemaphoreType.DMA
    return pl.pallas_call(
        functools.partial(kernel, n_row, n_col, n_dep, w),
        out_shape=(
            jax.ShapeDtypeStruct((block, width), bf16),
            jax.ShapeDtypeStruct((tokens_n, depth), bf16),
            jax.ShapeDtypeStruct((n_dep, n_col, rows, depth), bf16),
            jax.ShapeDtypeStruct((n_dep, n_row, block, share), bf16),
            jax.ShapeDtypeStruct((n_dep, n_row, block, share), bf16),
        ),
        in_specs=[vmem, hbm, hbm, vmem],
        out_specs=(vmem, vmem, hbm, hbm, hbm),
        scratch_shapes=[
            pltpu.VMEM((n_col, rows, depth), bf16),
            pltpu.VMEM((chunks, depth, lanes), bf16),
            pltpu.VMEM((chunks, n_row, block, lanes), bf16),
            pltpu.VMEM((chunks, n_row, block, lanes), bf16),
            pltpu.VMEM((chunks, n_row, block, lanes), bf16),
            pltpu.VMEM((chunks, n_row, block, lanes), bf16),
            pltpu.VMEM((tokens_n, depth), jnp.float32),
            dma((chunks, 2 * n_dep)),
            dma((n_col,)), dma((n_col,)), dma,
            dma((n_dep,)), dma((n_dep,)),
            dma((chunks, n_row)), dma((chunks, n_row)), dma((chunks, n_row)),
            dma((chunks, n_row)), dma((chunks, n_row)), dma((chunks, n_row)),
            dma((chunks, n_dep, 2)), dma((chunks, n_dep, 2)), dma((chunks, 2)),
        ],
        compiler_params=pltpu.CompilerParams(
            collective_id=0, has_side_effects=True, vmem_limit_bytes=60 * 1024 * 1024
        ),
        cost_estimate=pl.CostEstimate(
            flops=8 * tokens_n * depth * width,
            bytes_accessed=4 * depth * width,
            transcendentals=block * width,
        ),
    )(tokens, gate_weight, up_weight, cotangent)


def on_device(n_row, n_col, n_dep, tokens, gate_weight, up_weight, cotangent):
    depth = tokens.shape[1]
    hidden, part, all_tokens, all_gate, all_up = exchange(
        n_row, n_col, n_dep, tokens, gate_weight, up_weight, cotangent
    )
    grad_tokens = lax.psum_scatter(part, "col", scatter_dimension=0, tiled=True)
    share = all_gate.shape[3]
    contract = (((0,), (0,)), ((), ()))
    flat = all_tokens.reshape(-1, depth)
    sums = [
        lax.dot_general(
            flat, grad.reshape(-1, share), contract, preferred_element_type=jnp.float32
        ).astype(jnp.bfloat16)
        for grad in (all_gate, all_up)
    ]
    return (hidden, grad_tokens, *sums)


def solution(mesh):
    sizes = tuple(mesh.shape[axis] for axis in ("row", "col", "dep"))
    return jax.shard_map(
        functools.partial(on_device, *sizes),
        mesh=mesh,
        in_specs=(
            P(("dep", "col"), "row"),
            P("row", "col"),
            P("row", "col"),
            P(("dep", "row"), "col"),
        ),
        out_specs=(
            P(("dep", "row"), "col"),
            P(("dep", "col"), "row"),
            P("row", ("col", "dep")),
            P("row", ("col", "dep")),
        ),
        check_vma=False,
    )
```

time: 579 us -> 162 us (0.28)
  waiting for transfers between devices: 474 us -> 8.67 us
  Pallas kernels: 0 us -> 123 us
  matrix products: 64.2 us -> 15.5 us
  local copies, waits for them, and re-layouts: 20.1 us -> 0.78 us
    reduce_scatter x4 -> x1, waiting for transfers between devices: 377 us -> 8.66 us  [on_device(): grad_tokens = lax.psum_scatter(part, 'col', scatter_dimension=0, tiled=True)]
    pallas_call x0 -> x1, Pallas kernels: none -> 123 us  [exchange(): pl.pallas_call(functools.partial(kernel, n_row, n_col, n_dep, w), out_sha...]
    all_gather x3 -> x0, waiting for transfers between devices: 95.6 us -> none  [the longest x1 41.3 us: on_device(): lax.all_gather(grad_up, 'row', axis=0, tiled=True)]
    dot_general x6 -> x2, matrix products: 64.2 us -> 15.5 us  [on_device(): lax.dot_general(flat, grad.reshape(-1, share), contract, preferred_elemen...]
    unnamed x8 -> x7, local copies, waits for them, and re-layouts: 20.1 us -> 0.78 us
  transfers between devices with their start and end apart: 7 -> 1, of which waited for: 7 -> 1; matrix products, arithmetic and copies ran while one was open for 11% -> 10% of each run, Pallas kernels for 0% -> 0%
where the time goes in v2:
time: 162 us
  Pallas kernels  123 us (76%)
  matrix products  15.5 us (10%)
  between operations  14.1 us (9%)
  waiting for transfers between devices  8.67 us (5%)
    pallas_call x1, Pallas kernels, exchange(): pl.pallas_call(functools.partial(kernel, n_row, n_col, n_dep, w), out_sha...  123 us
    dot_general x2, matrix products, on_device(): lax.dot_general(flat, grad.reshape(-1, share), contract, preferred_elemen...  15.5 us
    reduce_scatter x1, waiting for transfers between devices, on_device(): grad_tokens = lax.psum_scatter(part, 'col', scatter_dimension=0, tiled=True)  8.66 us
  transfers between devices with their start and end apart: 1, of which 1 were waited for; matrix products, arithmetic and copies ran while one was open for 10% of the time, Pallas kernels for 0%

profile of v2, /device:TPU:0, one launch (start us, length us, event | category | flops | bytes accessed | tf_op | source)
XLA Modules:
  0.0 161.7 jit_solution(18183693896100875105)
XLA Ops:
  7.2 0.0 reduce-scatter.2.cloned.1.call-start
  7.2 122.6 %shard_map.75 = (bf16[64,3584]{1,0:T(8,128)(2,1)}, bf16[256,2048]{1,0:T(8,128)(2,1)}, bf16[2,4,64,2048]{3,2,1,0:T(8,128)(2,1)}, bf16[2,4,64,1792]{3,2,1,0:T(8,128)(2,1)}, bf16[2,4,64,1792]{3,2,1,0:T(8,128)(2,1)}) custom-call(bf16[64,2048]{1,0:T(8,128)(2,1)} %tokens_ref.1, bf16[2048,3584]{1,0:T(8,128)(2,1)} %gate_w_ref.1, bf16[2048,3584]{1,0:T(8,128)(2,1)} %up_w_ref.1, ...), custom_call_target="tpu_custom_call" | custom-call | flops 15032385536 | bytes 29360128 | tf_op jit(solution)/shard_map/pallas_call | solution.py:332
  129.9 0.0 reduce-scatter.2.cloned.1.call-update
  129.9 0.0 copy-start.1
  129.9 0.0 copy-start.2
  129.9 9.4 %bitcast_convert_fusion.1 = bf16[2048,1792]{1,0:T(8,128)(2,1)} fusion(bf16[2,4,64,2048]{3,2,1,0:T(8,128)(2,1)} %get-tuple-element.11, bf16[2,4,64,1792]{3,2,1,0:T(8,128)(2,1)} %get-tuple-element.12), kind=kOutput, calls=%fused_computation.1 | convolution fusion | flops 3761766400 | bytes 11272192 | tf_op jit(solution)/shard_map/dot_general | solution.py:379
  139.3 0.0 copy-done.1
  139.3 0.0 copy-done.2
  139.3 0.0 copy-start
  139.3 6.1 %bitcast_convert_fusion = bf16[2048,1792]{1,0:T(8,128)(2,1)} fusion(bf16[2,4,64,2048]{3,2,1,0:T(8,128)(2,1)S(1)} %copy-done.1, bf16[2,4,64,1792]{3,2,1,0:T(8,128)(2,1)S(1)} %copy-done.2), kind=kOutput, calls=%fused_computation | convolution fusion | flops 3761766400 | bytes 11272192 | tf_op jit(solution)/shard_map/dot_general | solution.py:379
  145.4 8.7 %reduce-scatter.2.cloned.1.call-done = bf16[64,2048]{1,0:T(8,128)(2,1)} async-done(((bf16[256,2048]{1,0:T(8,128)(2,1)}), bf16[64,2048]{1,0:T(8,128)(2,1)}) %reduce-scatter.2.cloned.1.call-update) | async-done | bytes 262160 | tf_op jit(solution)/shard_map/reduce_scatter | solution.py:374
  154.0 0.0 copy-done
  154.0 0.8 copy.11
Async XLA Ops:
  7.2 146.9 %reduce-scatter.2.cloned.1.call-start = ((), (), s32[]{:S(2)}) async-start(), calls=%async_computation.1 | async-start | bytes 1310720 | tf_op jit(solution)/shard_map/reduce_scatter | solution.py:374
  129.9 9.4 %copy-start.1 = (bf16[2,4,64,2048]{3,2,1,0:T(8,128)(2,1)S(1)}, bf16[2,4,64,2048]{3,2,1,0:T(8,128)(2,1)}, u32[]{:S(2)}) copy-start(bf16[2,4,64,2048]{3,2,1,0:T(8,128)(2,1)} %get-tuple-element.11) | copy-start | bytes 6291460
  129.9 9.4 %copy-start.2 = (bf16[2,4,64,1792]{3,2,1,0:T(8,128)(2,1)S(1)}, bf16[2,4,64,1792]{3,2,1,0:T(8,128)(2,1)}, u32[]{:S(2)}) copy-start(bf16[2,4,64,1792]{3,2,1,0:T(8,128)(2,1)} %get-tuple-element.13) | copy-start | bytes 5505028
  139.3 14.8 %copy-start = (bf16[64,3584]{1,0:T(8,128)(2,1)S(1)}, bf16[64,3584]{1,0:T(8,128)(2,1)}, u32[]{:S(2)}) copy-start(bf16[64,3584]{1,0:T(8,128)(2,1)} %get-tuple-element.18) | copy-start | bytes 1376260
Sparse Core Ops, SparseCore 0:
  130.0 23.9 reduce-scatter.1

commit v3 on v2

--- a/solution.py
+++ b/solution.py
@@ -9,6 +9,9 @@
 
 MESH = pl.DeviceIdType.MESH
 WIDTH = 128
+AHEAD = 2
+SUM_LAG = 1
+GATHER_LAG = 1
 
 
 def kernel(
@@ -74,6 +77,8 @@
     def _():
         pl.semaphore_wait(barrier, peers + 1)
 
+    other = my_col + 1 - 2 * lax.rem(my_col, 2)
+
     def token_copy(step):
         return pltpu.make_async_remote_copy(
             src_ref=tokens_ref, dst_ref=tok.at[my_col],
@@ -81,12 +86,28 @@
             device_id={"col": lax.rem(my_col + step, n_col)}, device_id_type=MESH,
         )
 
-    for step in range(1, n_col):
+    def pair_copy(step):
+        if step == 0:
+            src, at = tokens_ref, my_col
+        else:
+            at = lax.rem(my_col - step + n_col, n_col)
+            src = tok.at[at]
+        return pltpu.make_async_remote_copy(
+            src_ref=src, dst_ref=tok.at[at],
+            send_sem=tok_send.at[step + 1], recv_sem=tok_recv.at[step + 1],
+            device_id={"col": other}, device_id_type=MESH,
+        )
+
+    for step in range(2, n_col, 2):
         token_copy(step).start()
+    pair_copy(0).start()
     tok[pl.ds(my_col, 1)] = tokens_ref[...][None]
     acc[...] = jnp.zeros_like(acc)
-    for step in range(1, n_col):
+    for step in range(2, n_col, 2):
         token_copy(step).wait_recv()
+        pair_copy(step).start()
+    for step in range(0, n_col, 2):
+        pair_copy(step).wait_recv()
 
     def slice_copy(step):
         return pltpu.make_async_remote_copy(
@@ -143,6 +164,9 @@
             out_refs[k].at[my_dep, :, :, pl.ds(pl.multiple_of(c * w, w), w)],
             dep_local.at[c, k],
         )
+
+    def ready(j):
+        return (jnp.maximum(j, last - j) - 1) * SUM_LAG
 
     def valid(c):
         return jnp.logical_and(c >= 0, c < chunks)
@@ -163,7 +187,7 @@
         ref[...] = (ref[...].astype(jnp.float32) + other[...].astype(jnp.float32)).astype(jnp.bfloat16)
 
     def reduce_right(c):
-        for j in range(1, n_row):
+        for j in reversed(range(1, n_row)):
             @pl.when(j > me)
             def _():
                 @pl.when(me > 0)
@@ -221,10 +245,13 @@
 
     def relay(t):
         for away in range(1, n_row):
-            c = t - last - away
-
-            @pl.when(valid(c))
-            def _():
+            c_up = t - ready(me - away) - away * GATHER_LAG
+            c_down = t - ready(me + away) - away * GATHER_LAG
+
+            @pl.when(valid(c_up))
+            def _():
+                c = c_up
+
                 @pl.when(me - away >= 0)
                 def _():
                     ag_right(c, me - away).wait_recv()
@@ -232,6 +259,10 @@
                     @pl.when(me < last)
                     def _():
                         ag_right(c, me - away).start()
+
+            @pl.when(valid(c_down))
+            def _():
+                c = c_down
 
                 @pl.when(me + away <= last)
                 def _():
@@ -257,44 +288,7 @@
                 lhs, weights[c, rows, :], (((1,), (1,)), ((), ())), preferred_element_type=jnp.float32
             )
 
-    @pl.loop(0, chunks + 2 * last)
-    def _(t):
-        @pl.when(t < chunks)
-        def _():
-            forward(t)
-
-        c_right = t - me
-        @pl.when(valid(c_right))
-        def _():
-            reduce_right(c_right)
-
-        c_left = t - (last - me)
-        @pl.when(valid(c_left))
-        def _():
-            reduce_left(c_left)
-
-        relay(t)
-
-        c_own = t - last
-        @pl.when(valid(c_own))
-        def _():
-            finish(c_own)
-
-        c_back = t - last - jnp.maximum(me, last - me)
-        @pl.when(valid(c_back))
-        def _():
-            backward(c_back)
-
-    part_ref[...] = acc[...].astype(jnp.bfloat16)
-
-    for step in range(1, n_col):
-        token_copy(step).wait_send()
-    for step in range(1, n_dep):
-        slice_copy(step).wait()
-    tok_out.wait()
-
-    @pl.loop(0, chunks)
-    def _(c):
+    def retire(c):
         for j in range(n_row):
             @pl.when(j > me)
             def _():
@@ -315,6 +309,71 @@
             for step in range(1, n_dep):
                 dep_copy(c, step, k).wait()
             dep_own(c, k).wait()
+
+    def start(c):
+        forward(c)
+
+        @pl.when(me == 0)
+        def _():
+            reduce_right(c)
+
+        @pl.when(me == last)
+        def _():
+            reduce_left(c)
+
+    @pl.loop(0, AHEAD)
+    def _(c):
+        start(c)
+
+    length = (last - 1) * SUM_LAG + last * GATHER_LAG
+    done = 0
+    for j in range(n_row):
+        at = (max(j, last - j) - 1) * SUM_LAG
+        done = jnp.maximum(done, at + jnp.abs(me - j) * GATHER_LAG)
+
+    @pl.loop(0, chunks + length)
+    def _(t):
+        @pl.when(t + AHEAD < chunks)
+        def _():
+            start(t + AHEAD)
+
+        c_right = t - (me - 1) * SUM_LAG
+        @pl.when(jnp.logical_and(valid(c_right), me > 0))
+        def _():
+            reduce_right(c_right)
+
+        c_left = t - (last - me - 1) * SUM_LAG
+        @pl.when(jnp.logical_and(valid(c_left), me < last))
+        def _():
+            reduce_left(c_left)
+
+        c_own = t - ready(me)
+        @pl.when(valid(c_own))
+        def _():
+            finish(c_own)
+
+        relay(t)
+
+        c_back = t - done
+        @pl.when(valid(c_back))
+        def _():
+            backward(c_back)
+
+        c_out = t - length - 1
+        @pl.when(valid(c_out))
+        def _():
+            retire(c_out)
+
+    part_ref[...] = acc[...].astype(jnp.bfloat16)
+    retire(chunks - 1)
+
+    for step in range(2, n_col, 2):
+        token_copy(step).wait_send()
+    for step in range(0, n_col, 2):
+        pair_copy(step).wait_send()
+    for step in range(1, n_dep):
+        slice_copy(step).wait()
+    tok_out.wait()
 
 
 def exchange(n_row, n_col, n_dep, tokens, gate_weight, up_weight, cotangent):
@@ -371,7 +430,13 @@
     hidden, part, all_tokens, all_gate, all_up = exchange(
         n_row, n_col, n_dep, tokens, gate_weight, up_weight, cotangent
     )
-    grad_tokens = lax.psum_scatter(part, "col", scatter_dimension=0, tiled=True)
+    me = lax.axis_index("col")
+    rows = tokens.shape[0]
+    terms = [lax.dynamic_slice_in_dim(part, me * rows, rows, 0)]
+    for step in range(1, n_col):
+        block = lax.dynamic_slice_in_dim(part, lax.rem(me + step, n_col) * rows, rows, 0)
+        terms.append(lax.ppermute(block, "col", [(i, (i + step) % n_col) for i in range(n_col)]))
+    grad_tokens = sum(term.astype(jnp.float32) for term in terms).astype(jnp.bfloat16)
     share = all_gate.shape[3]
     contract = (((0,), (0,)), ((), ()))
     flat = all_tokens.reshape(-1, depth)

time: 162 us -> 148 us (0.914)
  between operations: 14.1 us -> 0.69 us
  waiting for transfers between devices: 8.67 us -> 0.01 us
  starting transfers between devices: 0.04 us -> 3.44 us
  other arithmetic: 0 us -> 1.79 us
    reduce_scatter x1 -> x0, waiting for transfers between devices: 8.66 us -> none  [on_device(): grad_tokens = lax.psum_scatter(part, 'col', scatter_dimension=0, tiled=True)]
    ppermute x0 -> x3, starting transfers between devices: none -> 3.44 us  [on_device(): lax.ppermute(block, 'col', [(i, (i + step) % n_col) for i in range(n_col)])]
    convert_element_type x0 -> x1, other arithmetic: none -> 1.79 us  [on_device(): sum((term.astype(jnp.float32) for term in terms)).astype(jnp.bfloat16)]
    pallas_call x1, Pallas kernels: 123 us -> 124 us  [exchange(): pl.pallas_call(functools.partial(kernel, n_row, n_col, n_dep, w), out_sha...]
  transfers between devices with their start and end apart: 1 -> 3, of which waited for: 1 -> 0; matrix products, arithmetic and copies ran while one was open for 10% -> 10% of each run, Pallas kernels for 0% -> 0%
where the time goes in v3:
time: 148 us
  Pallas kernels  124 us (84%)
  matrix products  15.5 us (10%)
  starting transfers between devices  3.44 us (2%)
  local copies, waits for them, and re-layouts  1.95 us (1%)
  other arithmetic  1.79 us (1%)
    pallas_call x1, Pallas kernels, exchange(): pl.pallas_call(functools.partial(kernel, n_row, n_col, n_dep, w), out_sha...  124 us
    dot_general x2, matrix products, on_device(): lax.dot_general(flat, grad.reshape(-1, share), contract, preferred_elemen...  15.5 us
    ppermute x3, starting transfers between devices, on_device(): lax.ppermute(block, 'col', [(i, (i + step) % n_col) for i in range(n_col)])  3.44 us
  transfers between devices with their start and end apart: 3, of which 0 were waited for; matrix products, arithmetic and copies ran while one was open for 10% of the time, Pallas kernels for 0%

profile of v3, /device:TPU:0, one launch (start us, length us, event | category | flops | bytes accessed | tf_op | source)
XLA Modules:
  0.0 147.7 jit_solution(5231736200266660288)
XLA Ops:
  0.7 124.3 %shard_map.75 = (bf16[64,3584]{1,0:T(8,128)(2,1)}, bf16[256,2048]{1,0:T(8,128)(2,1)}, bf16[2,4,64,2048]{3,2,1,0:T(8,128)(2,1)}, bf16[2,4,64,1792]{3,2,1,0:T(8,128)(2,1)}, bf16[2,4,64,1792]{3,2,1,0:T(8,128)(2,1)}) custom-call(bf16[64,2048]{1,0:T(8,128)(2,1)} %tokens_ref.1, bf16[2048,3584]{1,0:T(8,128)(2,1)} %gate_w_ref.1, bf16[2048,3584]{1,0:T(8,128)(2,1)} %up_w_ref.1, ...), custom_call_target="tpu_custom_call" | custom-call | flops 15032385536 | bytes 29360128 | tf_op jit(solution)/shard_map/pallas_call | solution.py:391
  125.0 1.2 constant_dynamic-slice_fusion.2
  126.2 0.1 collective-permute-start
  126.2 1.7 %collective-permute-start.2 = (bf16[64,2048]{1,0:T(8,128)(2,1)S(1)}, bf16[64,2048]{1,0:T(8,128)(2,1)S(1)}, u32[]{:S(2)}, u32[]{:S(2)}) collective-permute-start(bf16[64,2048]{1,0:T(8,128)(2,1)S(1)} %get-tuple-element.15), channel_id=1, source_target_pairs={{0,6},{2,0},{4,2},{6,4},{1,7},{3,1},{5,3},{7,5},{8,14},{10,8},{12,... | collective-permute-start | bytes 786440 | tf_op jit(solution)/shard_map/ppermute | solution.py:438
  128.0 1.7 %collective-permute-start.1 = (bf16[64,2048]{1,0:T(8,128)(2,1)S(1)}, bf16[64,2048]{1,0:T(8,128)(2,1)S(1)}, u32[]{:S(2)}, u32[]{:S(2)}) collective-permute-start(bf16[64,2048]{1,0:T(8,128)(2,1)S(1)} %get-tuple-element.16), channel_id=1, source_target_pairs={{0,4},{2,6},{4,0},{6,2},{1,5},{3,7},{5,1},{7,3},{8,12},{10,14},{12... | collective-permute-start | bytes 786440 | tf_op jit(solution)/shard_map/ppermute | solution.py:438
  129.6 0.0 copy-start.1
  129.6 0.0 copy-start.2
  129.6 9.4 %bitcast_convert_fusion.1 = bf16[2048,1792]{1,0:T(8,128)(2,1)} fusion(bf16[2,4,64,2048]{3,2,1,0:T(8,128)(2,1)} %get-tuple-element.11, bf16[2,4,64,1792]{3,2,1,0:T(8,128)(2,1)} %get-tuple-element.12), kind=kOutput, calls=%fused_computation.1 | convolution fusion | flops 3761766400 | bytes 11272192 | tf_op jit(solution)/shard_map/dot_general | solution.py:444
  139.0 0.0 copy-done.1
  139.0 0.0 copy-done.2
  139.0 0.0 copy-start
  139.0 6.1 %bitcast_convert_fusion = bf16[2048,1792]{1,0:T(8,128)(2,1)} fusion(bf16[2,4,64,2048]{3,2,1,0:T(8,128)(2,1)S(1)} %copy-done.1, bf16[2,4,64,1792]{3,2,1,0:T(8,128)(2,1)S(1)} %copy-done.2), kind=kOutput, calls=%fused_computation | convolution fusion | flops 3761766400 | bytes 11272192 | tf_op jit(solution)/shard_map/dot_general | solution.py:444
  145.1 0.0 collective-permute-done
  145.1 0.0 collective-permute-done.2
  145.1 0.0 collective-permute-done.1
  145.1 1.8 %add_convert_fusion = bf16[64,2048]{1,0:T(8,128)(2,1)} fusion(bf16[64,2048]{1,0:T(8,128)(2,1)S(1)} %collective-permute-done.2, bf16[64,2048]{1,0:T(8,128)(2,1)S(1)} %collective-permute-done.1, bf16[64,2048]{1,0:T(8,128)(2,1)S(1)} %collective-permute-done, bf16[256,2048]{1,0:T(8,128)(2,1)} %get-tuple-element.10, s32[]{:T(128)S(6)} %select_n.12), kind=kLoop, calls=%fused_computation.2 | loop fusion | flops 1048576 | bytes 1310724 | tf_op jit(solution)/shard_map/convert_element_type | solution.py:439
  146.9 0.0 copy-done
  146.9 0.8 copy.11
Async XLA Ops:
  126.2 18.9 %collective-permute-start = (bf16[64,2048]{1,0:T(8,128)(2,1)S(1)}, bf16[64,2048]{1,0:T(8,128)(2,1)S(1)}, u32[]{:S(2)}, u32[]{:S(2)}) collective-permute-start(bf16[64,2048]{1,0:T(8,128)(2,1)S(1)} %get-tuple-element.14), channel_id=1, source_target_pairs={{0,2},{2,4},{4,6},{6,0},{1,3},{3,5},{5,7},{7,1},{8,10},{10,12},{12... | collective-permute-start | bytes 786440 | tf_op jit(solution)/shard_map/ppermute | solution.py:438
  126.2 18.9 %collective-permute-start.2 = (bf16[64,2048]{1,0:T(8,128)(2,1)S(1)}, bf16[64,2048]{1,0:T(8,128)(2,1)S(1)}, u32[]{:S(2)}, u32[]{:S(2)}) collective-permute-start(bf16[64,2048]{1,0:T(8,128)(2,1)S(1)} %get-tuple-element.15), channel_id=1, source_target_pairs={{0,6},{2,0},{4,2},{6,4},{1,7},{3,1},{5,3},{7,5},{8,14},{10,8},{12,... | collective-permute-start | bytes 786440 | tf_op jit(solution)/shard_map/ppermute | solution.py:438
  128.0 17.1 %collective-permute-start.1 = (bf16[64,2048]{1,0:T(8,128)(2,1)S(1)}, bf16[64,2048]{1,0:T(8,128)(2,1)S(1)}, u32[]{:S(2)}, u32[]{:S(2)}) collective-permute-start(bf16[64,2048]{1,0:T(8,128)(2,1)S(1)} %get-tuple-element.16), channel_id=1, source_target_pairs={{0,4},{2,6},{4,0},{6,2},{1,5},{3,7},{5,1},{7,3},{8,12},{10,14},{12... | collective-permute-start | bytes 786440 | tf_op jit(solution)/shard_map/ppermute | solution.py:438
  129.6 9.4 %copy-start.1 = (bf16[2,4,64,2048]{3,2,1,0:T(8,128)(2,1)S(1)}, bf16[2,4,64,2048]{3,2,1,0:T(8,128)(2,1)}, u32[]{:S(2)}) copy-start(bf16[2,4,64,2048]{3,2,1,0:T(8,128)(2,1)} %get-tuple-element.11) | copy-start | bytes 6291460
  129.6 9.4 %copy-start.2 = (bf16[2,4,64,1792]{3,2,1,0:T(8,128)(2,1)S(1)}, bf16[2,4,64,1792]{3,2,1,0:T(8,128)(2,1)}, u32[]{:S(2)}) copy-start(bf16[2,4,64,1792]{3,2,1,0:T(8,128)(2,1)} %get-tuple-element.13) | copy-start | bytes 5505028
  139.0 7.9 %copy-start = (bf16[64,3584]{1,0:T(8,128)(2,1)S(1)}, bf16[64,3584]{1,0:T(8,128)(2,1)}, u32[]{:S(2)}) copy-start(bf16[64,3584]{1,0:T(8,128)(2,1)} %get-tuple-element.21) | copy-start | bytes 1376260

commit v4 on v3

--- a/solution.py
+++ b/solution.py
@@ -12,6 +12,7 @@
 AHEAD = 2
 SUM_LAG = 1
 GATHER_LAG = 1
+LOADED = 3
 
 
 def kernel(
@@ -48,10 +49,6 @@
             for k in range(2):
                 weight_copy(c, h, k).start()
 
-    @pl.loop(0, chunks)
-    def _(c):
-        load_weights(c)
-
     barrier = pltpu.get_barrier_semaphore()
     for step in range(1, n_col):
         pl.semaphore_signal(barrier, inc=1, device_id={"col": lax.rem(my_col + step, n_col)}, device_id_type=MESH)
@@ -101,6 +98,11 @@
     for step in range(2, n_col, 2):
         token_copy(step).start()
     pair_copy(0).start()
+
+    @pl.loop(0, LOADED)
+    def _(c):
+        load_weights(c)
+
     tok[pl.ds(my_col, 1)] = tokens_ref[...][None]
     acc[...] = jnp.zeros_like(acc)
     for step in range(2, n_col, 2):
@@ -278,14 +280,14 @@
                 dep_copy(c, step, k).start()
         for k in range(2):
             dep_own(c, k).start()
-        lhs = grads[c].reshape(tokens_n, lanes)
+        rhs = grads[c].reshape(tokens_n, lanes)
         tile = min(512, depth)
 
         @pl.loop(0, depth // tile)
         def _(i):
             rows = pl.ds(pl.multiple_of(i * tile, tile), tile)
-            acc[:, rows] += lax.dot_general(
-                lhs, weights[c, rows, :], (((1,), (1,)), ((), ())), preferred_element_type=jnp.float32
+            acc[rows] += lax.dot_general(
+                weights[c, rows, :], rhs, (((1,), (1,)), ((), ())), preferred_element_type=jnp.float32
             )
 
     def retire(c):
@@ -311,6 +313,10 @@
             dep_own(c, k).wait()
 
     def start(c):
+        @pl.when(c + LOADED < chunks)
+        def _():
+            load_weights(c + LOADED)
+
         forward(c)
 
         @pl.when(me == 0)
@@ -364,7 +370,9 @@
         def _():
             retire(c_out)
 
-    part_ref[...] = acc[...].astype(jnp.bfloat16)
+    tile = min(256, depth)
+    for at in range(0, depth, tile):
+        part_ref[:, at:at + tile] = acc[at:at + tile].T.astype(jnp.bfloat16)
     retire(chunks - 1)
 
     for step in range(2, n_col, 2):
@@ -406,7 +414,7 @@
             pltpu.VMEM((chunks, n_row, block, lanes), bf16),
             pltpu.VMEM((chunks, n_row, block, lanes), bf16),
             pltpu.VMEM((chunks, n_row, block, lanes), bf16),
-            pltpu.VMEM((tokens_n, depth), jnp.float32),
+            pltpu.VMEM((depth, tokens_n), jnp.float32),
             dma((chunks, 2 * n_dep)),
             dma((n_col,)), dma((n_col,)), dma,
             dma((n_dep,)), dma((n_dep,)),

time: 148 us -> 148 us (level)
  no operation moved by 1% of the time
where the time goes in v4:
time: 148 us
  Pallas kernels  124 us (84%)
  matrix products  15.5 us (10%)
  starting transfers between devices  3.45 us (2%)
  local copies, waits for them, and re-layouts  1.95 us (1%)
  other arithmetic  1.79 us (1%)
    pallas_call x1, Pallas kernels, exchange(): pl.pallas_call(functools.partial(kernel, n_row, n_col, n_dep, w), out_sha...  124 us
    dot_general x2, matrix products, on_device(): lax.dot_general(flat, grad.reshape(-1, share), contract, preferred_elemen...  15.5 us
    ppermute x3, starting transfers between devices, on_device(): lax.ppermute(block, 'col', [(i, (i + step) % n_col) for i in range(n_col)])  3.45 us
  transfers between devices with their start and end apart: 3, of which 0 were waited for; matrix products, arithmetic and copies ran while one was open for 10% of the time, Pallas kernels for 0%

profile of v4, /device:TPU:0, one launch (start us, length us, event | category | flops | bytes accessed | tf_op | source)
XLA Modules:
  0.0 147.5 jit_solution(1711846757723276766)
XLA Ops:
  0.7 124.2 %shard_map.75 = (bf16[64,3584]{1,0:T(8,128)(2,1)}, bf16[256,2048]{1,0:T(8,128)(2,1)}, bf16[2,4,64,2048]{3,2,1,0:T(8,128)(2,1)}, bf16[2,4,64,1792]{3,2,1,0:T(8,128)(2,1)}, bf16[2,4,64,1792]{3,2,1,0:T(8,128)(2,1)}) custom-call(bf16[64,2048]{1,0:T(8,128)(2,1)} %tokens_ref.1, bf16[2048,3584]{1,0:T(8,128)(2,1)} %gate_w_ref.1, bf16[2048,3584]{1,0:T(8,128)(2,1)} %up_w_ref.1, ...), custom_call_target="tpu_custom_call" | custom-call | flops 15032385536 | bytes 29360128 | tf_op jit(solution)/shard_map/pallas_call | solution.py:399
  124.8 1.2 constant_dynamic-slice_fusion.2
  126.0 0.1 collective-permute-start
  126.1 1.7 %collective-permute-start.2 = (bf16[64,2048]{1,0:T(8,128)(2,1)S(1)}, bf16[64,2048]{1,0:T(8,128)(2,1)S(1)}, u32[]{:S(2)}, u32[]{:S(2)}) collective-permute-start(bf16[64,2048]{1,0:T(8,128)(2,1)S(1)} %get-tuple-element.15), channel_id=1, source_target_pairs={{0,6},{2,0},{4,2},{6,4},{1,7},{3,1},{5,3},{7,5},{8,14},{10,8},{12,... | collective-permute-start | bytes 786440 | tf_op jit(solution)/shard_map/ppermute | solution.py:446
  127.8 1.7 %collective-permute-start.1 = (bf16[64,2048]{1,0:T(8,128)(2,1)S(1)}, bf16[64,2048]{1,0:T(8,128)(2,1)S(1)}, u32[]{:S(2)}, u32[]{:S(2)}) collective-permute-start(bf16[64,2048]{1,0:T(8,128)(2,1)S(1)} %get-tuple-element.16), channel_id=1, source_target_pairs={{0,4},{2,6},{4,0},{6,2},{1,5},{3,7},{5,1},{7,3},{8,12},{10,14},{12... | collective-permute-start | bytes 786440 | tf_op jit(solution)/shard_map/ppermute | solution.py:446
  129.5 0.0 copy-start.1
  129.5 0.0 copy-start.2
  129.5 9.4 %bitcast_convert_fusion.1 = bf16[2048,1792]{1,0:T(8,128)(2,1)} fusion(bf16[2,4,64,2048]{3,2,1,0:T(8,128)(2,1)} %get-tuple-element.11, bf16[2,4,64,1792]{3,2,1,0:T(8,128)(2,1)} %get-tuple-element.12), kind=kOutput, calls=%fused_computation.1 | convolution fusion | flops 3761766400 | bytes 11272192 | tf_op jit(solution)/shard_map/dot_general | solution.py:452
  138.8 0.0 copy-done.1
  138.8 0.0 copy-done.2
  138.8 0.0 copy-start
  138.8 6.1 %bitcast_convert_fusion = bf16[2048,1792]{1,0:T(8,128)(2,1)} fusion(bf16[2,4,64,2048]{3,2,1,0:T(8,128)(2,1)S(1)} %copy-done.1, bf16[2,4,64,1792]{3,2,1,0:T(8,128)(2,1)S(1)} %copy-done.2), kind=kOutput, calls=%fused_computation | convolution fusion | flops 3761766400 | bytes 11272192 | tf_op jit(solution)/shard_map/dot_general | solution.py:452
  144.9 0.0 collective-permute-done
  144.9 0.0 collective-permute-done.2
  144.9 0.0 collective-permute-done.1
  144.9 1.8 %add_convert_fusion = bf16[64,2048]{1,0:T(8,128)(2,1)} fusion(bf16[64,2048]{1,0:T(8,128)(2,1)S(1)} %collective-permute-done.2, bf16[64,2048]{1,0:T(8,128)(2,1)S(1)} %collective-permute-done.1, bf16[64,2048]{1,0:T(8,128)(2,1)S(1)} %collective-permute-done, bf16[256,2048]{1,0:T(8,128)(2,1)} %get-tuple-element.10, s32[]{:T(128)S(6)} %select_n.12), kind=kLoop, calls=%fused_computation.2 | loop fusion | flops 1048576 | bytes 1310724 | tf_op jit(solution)/shard_map/convert_element_type | solution.py:447
  146.7 0.0 copy-done
  146.7 0.8 copy.11
Async XLA Ops:
  126.0 18.9 %collective-permute-start = (bf16[64,2048]{1,0:T(8,128)(2,1)S(1)}, bf16[64,2048]{1,0:T(8,128)(2,1)S(1)}, u32[]{:S(2)}, u32[]{:S(2)}) collective-permute-start(bf16[64,2048]{1,0:T(8,128)(2,1)S(1)} %get-tuple-element.14), channel_id=1, source_target_pairs={{0,2},{2,4},{4,6},{6,0},{1,3},{3,5},{5,7},{7,1},{8,10},{10,12},{12... | collective-permute-start | bytes 786440 | tf_op jit(solution)/shard_map/ppermute | solution.py:446
  126.1 18.9 %collective-permute-start.2 = (bf16[64,2048]{1,0:T(8,128)(2,1)S(1)}, bf16[64,2048]{1,0:T(8,128)(2,1)S(1)}, u32[]{:S(2)}, u32[]{:S(2)}) collective-permute-start(bf16[64,2048]{1,0:T(8,128)(2,1)S(1)} %get-tuple-element.15), channel_id=1, source_target_pairs={{0,6},{2,0},{4,2},{6,4},{1,7},{3,1},{5,3},{7,5},{8,14},{10,8},{12,... | collective-permute-start | bytes 786440 | tf_op jit(solution)/shard_map/ppermute | solution.py:446
  127.8 17.1 %collective-permute-start.1 = (bf16[64,2048]{1,0:T(8,128)(2,1)S(1)}, bf16[64,2048]{1,0:T(8,128)(2,1)S(1)}, u32[]{:S(2)}, u32[]{:S(2)}) collective-permute-start(bf16[64,2048]{1,0:T(8,128)(2,1)S(1)} %get-tuple-element.16), channel_id=1, source_target_pairs={{0,4},{2,6},{4,0},{6,2},{1,5},{3,7},{5,1},{7,3},{8,12},{10,14},{12... | collective-permute-start | bytes 786440 | tf_op jit(solution)/shard_map/ppermute | solution.py:446
  129.5 9.4 %copy-start.1 = (bf16[2,4,64,2048]{3,2,1,0:T(8,128)(2,1)S(1)}, bf16[2,4,64,2048]{3,2,1,0:T(8,128)(2,1)}, u32[]{:S(2)}) copy-start(bf16[2,4,64,2048]{3,2,1,0:T(8,128)(2,1)} %get-tuple-element.11) | copy-start | bytes 6291460
  129.5 9.4 %copy-start.2 = (bf16[2,4,64,1792]{3,2,1,0:T(8,128)(2,1)S(1)}, bf16[2,4,64,1792]{3,2,1,0:T(8,128)(2,1)}, u32[]{:S(2)}) copy-start(bf16[2,4,64,1792]{3,2,1,0:T(8,128)(2,1)} %get-tuple-element.13) | copy-start | bytes 5505028
  138.8 7.9 %copy-start = (bf16[64,3584]{1,0:T(8,128)(2,1)S(1)}, bf16[64,3584]{1,0:T(8,128)(2,1)}, u32[]{:S(2)}) copy-start(bf16[64,3584]{1,0:T(8,128)(2,1)} %get-tuple-element.21) | copy-start | bytes 1376260

commit v5 on v4

--- a/solution.py
+++ b/solution.py
@@ -11,7 +11,7 @@
 WIDTH = 128
 AHEAD = 2
 SUM_LAG = 1
-GATHER_LAG = 1
+GATHER_LAG = 2
 LOADED = 3
 
 
@@ -19,7 +19,7 @@
     n_row, n_col, n_dep, w,
     tokens_ref, gate_w_ref, up_w_ref, cot_ref,
     hidden_ref, part_ref, all_tok_ref, all_gate_ref, all_up_ref,
-    tok, weights, own, from_left, from_right, grads, acc,
+    tok, turned, weights, own, from_left, from_right, grads, acc,
     w_sem, tok_send, tok_recv, tok_local, slice_send, slice_recv,
     rs_send, left_recv, right_recv, ag_right_send, ag_left_send, ag_recv,
     dep_send, dep_recv, dep_local,
@@ -113,15 +113,21 @@
 
     def slice_copy(step):
         return pltpu.make_async_remote_copy(
-            src_ref=tok, dst_ref=all_tok_ref.at[my_dep],
+            src_ref=turned, dst_ref=all_tok_ref.at[my_dep],
             send_sem=slice_send.at[step], recv_sem=slice_recv.at[step],
             device_id={"dep": lax.rem(my_dep + step, n_dep)}, device_id_type=MESH,
         )
 
-    tok_out = pltpu.make_async_copy(tok, all_tok_ref.at[my_dep], tok_local)
-    for step in range(1, n_dep):
-        slice_copy(step).start()
-    tok_out.start()
+    tok_out = pltpu.make_async_copy(turned, all_tok_ref.at[my_dep], tok_local)
+
+    def turn():
+        tile = min(256, depth)
+        for at in range(0, depth, tile):
+            piece = tok[:, :, at:at + tile].reshape(tokens_n, tile)
+            turned[at:at + tile] = piece.astype(jnp.float32).T.astype(jnp.bfloat16)
+        for step in range(1, n_dep):
+            slice_copy(step).start()
+        tok_out.start()
 
     def rs_right(c, j):
         return pltpu.make_async_remote_copy(
@@ -359,6 +365,10 @@
             finish(c_own)
 
         relay(t)
+
+        @pl.when(t == 1)
+        def _():
+            turn()
 
         c_back = t - done
         @pl.when(valid(c_back))
@@ -401,7 +411,7 @@
         out_shape=(
             jax.ShapeDtypeStruct((block, width), bf16),
             jax.ShapeDtypeStruct((tokens_n, depth), bf16),
-            jax.ShapeDtypeStruct((n_dep, n_col, rows, depth), bf16),
+            jax.ShapeDtypeStruct((n_dep, depth, tokens_n), bf16),
             jax.ShapeDtypeStruct((n_dep, n_row, block, share), bf16),
             jax.ShapeDtypeStruct((n_dep, n_row, block, share), bf16),
         ),
@@ -409,6 +419,7 @@
         out_specs=(vmem, vmem, hbm, hbm, hbm),
         scratch_shapes=[
             pltpu.VMEM((n_col, rows, depth), bf16),
+            pltpu.VMEM((depth, tokens_n), bf16),
             pltpu.VMEM((chunks, depth, lanes), bf16),
             pltpu.VMEM((chunks, n_row, block, lanes), bf16),
             pltpu.VMEM((chunks, n_row, block, lanes), bf16),
@@ -433,6 +444,42 @@
     )(tokens, gate_weight, up_weight, cotangent)
 
 
+def weight_grad_kernel(tokens_ref, gate_ref, up_ref, gate_out, up_out):
+    n_dep, depth, _ = tokens_ref.shape
+    tile = min(512, depth)
+    for grad_ref, out_ref in ((gate_ref, gate_out), (up_ref, up_out)):
+        for at in range(0, depth, tile):
+            total = jnp.dot(tokens_ref[0, at:at + tile], grad_ref[0], preferred_element_type=jnp.float32)
+            for d in range(1, n_dep):
+                total = total + jnp.dot(
+                    tokens_ref[d, at:at + tile], grad_ref[d], preferred_element_type=jnp.float32
+                )
+            out_ref[at:at + tile] = total.astype(jnp.bfloat16)
+
+
+def weight_grads(turned, all_gate, all_up):
+    n_dep, depth, tokens_n = turned.shape
+    share = all_gate.shape[3]
+    wide = 256 if share % 256 == 0 else 128
+    grads = [g.reshape(n_dep, tokens_n, share) for g in (all_gate, all_up)]
+    taken = pl.BlockSpec((n_dep, tokens_n, wide), lambda i: (0, 0, i))
+    given = pl.BlockSpec((depth, wide), lambda i: (0, i))
+    shape = jax.ShapeDtypeStruct((depth, share), jnp.bfloat16)
+    return pl.pallas_call(
+        weight_grad_kernel,
+        grid=(share // wide,),
+        in_specs=[pl.BlockSpec((n_dep, depth, tokens_n), lambda i: (0, 0, 0)), taken, taken],
+        out_specs=(given, given),
+        out_shape=(shape, shape),
+        compiler_params=pltpu.CompilerParams(vmem_limit_bytes=48 * 1024 * 1024),
+        cost_estimate=pl.CostEstimate(
+            flops=4 * n_dep * tokens_n * depth * share,
+            bytes_accessed=4 * depth * share + 4 * n_dep * tokens_n * share,
+            transcendentals=0,
+        ),
+    )(turned, *grads)
+
+
 def on_device(n_row, n_col, n_dep, tokens, gate_weight, up_weight, cotangent):
     depth = tokens.shape[1]
     hidden, part, all_tokens, all_gate, all_up = exchange(
@@ -445,15 +492,7 @@
         block = lax.dynamic_slice_in_dim(part, lax.rem(me + step, n_col) * rows, rows, 0)
         terms.append(lax.ppermute(block, "col", [(i, (i + step) % n_col) for i in range(n_col)]))
     grad_tokens = sum(term.astype(jnp.float32) for term in terms).astype(jnp.bfloat16)
-    share = all_gate.shape[3]
-    contract = (((0,), (0,)), ((), ()))
-    flat = all_tokens.reshape(-1, depth)
-    sums = [
-        lax.dot_general(
-            flat, grad.reshape(-1, share), contract, preferred_element_type=jnp.float32
-        ).astype(jnp.bfloat16)
-        for grad in (all_gate, all_up)
-    ]
+    sums = weight_grads(all_tokens, all_gate, all_up)
     return (hidden, grad_tokens, *sums)
 
 

time: 148 us -> 147 us (level)
  matrix products: 15.5 us -> 0 us
  Pallas kernels: 124 us -> 134 us
  local copies, waits for them, and re-layouts: 1.95 us -> 6.53 us
    dot_general x2 -> x0, matrix products: 15.5 us -> none  [on_device(): lax.dot_general(flat, grad.reshape(-1, share), contract, preferred_elemen...]
    pallas_call x0 -> x1, Pallas kernels: none -> 10.1 us  [weight_grads(): pl.pallas_call(weight_grad_kernel, grid=(share // wide,), in_specs=[pl.Bl...]
    unnamed x7 -> x9, local copies, waits for them, and re-layouts: 0.78 us -> 5.36 us
  transfers between devices with their start and end apart: 3 -> 3, of which waited for: 0 -> 0; matrix products, arithmetic and copies ran while one was open for 10% -> 0% of each run, Pallas kernels for 0% -> 7%
where the time goes in v5:
time: 147 us
  Pallas kernels  134 us (91%)
  local copies, waits for them, and re-layouts  6.53 us (4%)
  starting transfers between devices  3.6 us (2%)
  other arithmetic  1.79 us (1%)
    pallas_call x1, Pallas kernels, exchange(): pl.pallas_call(functools.partial(kernel, n_row, n_col, n_dep, w), out_sha...  124 us
    pallas_call x1, Pallas kernels, weight_grads(): pl.pallas_call(weight_grad_kernel, grid=(share // wide,), in_specs=[pl.Bl...  10.1 us
    unnamed x9, local copies, waits for them, and re-layouts  5.36 us
    ppermute x3, starting transfers between devices, on_device(): lax.ppermute(block, 'col', [(i, (i + step) % n_col) for i in range(n_col)])  3.6 us
  transfers between devices with their start and end apart: 3, of which 0 were waited for; matrix products, arithmetic and copies ran while one was open for 0% of the time, Pallas kernels for 7%

profile of v5, /device:TPU:0, one launch (start us, length us, event | category | flops | bytes accessed | tf_op | source)
XLA Modules:
  0.0 146.8 jit_solution(5453518590723136604)
XLA Ops:
  0.7 124.1 %shard_map.75 = (bf16[64,3584]{1,0:T(8,128)(2,1)}, bf16[256,2048]{1,0:T(8,128)(2,1)}, bf16[2,2048,256]{2,1,0:T(8,128)(2,1)}, bf16[2,4,64,1792]{3,2,1,0:T(8,128)(2,1)}, bf16[2,4,64,1792]{3,2,1,0:T(8,128)(2,1)}) custom-call(bf16[64,2048]{1,0:T(8,128)(2,1)} %tokens_ref.1, bf16[2048,3584]{1,0:T(8,128)(2,1)} %gate_w_ref.1, bf16[2048,3584]{1,0:T(8,128)(2,1)} %up_w_ref.1, ...), custom_call_target="tpu_custom_call" | custom-call | flops 15032385536 | bytes 29360128 | tf_op jit(solution)/shard_map/pallas_call | solution.py:409
  124.7 1.2 constant_dynamic-slice_fusion.2
  125.9 0.1 collective-permute-start
  126.0 1.7 %collective-permute-start.2 = (bf16[64,2048]{1,0:T(8,128)(2,1)S(1)}, bf16[64,2048]{1,0:T(8,128)(2,1)S(1)}, u32[]{:S(2)}, u32[]{:S(2)}) collective-permute-start(bf16[64,2048]{1,0:T(8,128)(2,1)S(1)} %get-tuple-element.19), channel_id=1, source_target_pairs={{0,6},{2,0},{4,2},{6,4},{1,7},{3,1},{5,3},{7,5},{8,14},{10,8},{12,... | collective-permute-start | bytes 786440 | tf_op jit(solution)/shard_map/ppermute | solution.py:493
  127.7 1.8 %collective-permute-start.1 = (bf16[64,2048]{1,0:T(8,128)(2,1)S(1)}, bf16[64,2048]{1,0:T(8,128)(2,1)S(1)}, u32[]{:S(2)}, u32[]{:S(2)}) collective-permute-start(bf16[64,2048]{1,0:T(8,128)(2,1)S(1)} %get-tuple-element.20), channel_id=1, source_target_pairs={{0,4},{2,6},{4,0},{6,2},{1,5},{3,7},{5,1},{7,3},{8,12},{10,14},{12... | collective-permute-start | bytes 786440 | tf_op jit(solution)/shard_map/ppermute | solution.py:493
  129.5 0.0 copy-start
  129.5 1.5 %copy-done = bf16[2,4,64,1792]{3,2,1,0:T(8,128)(2,1)S(1)} copy-done((bf16[2,4,64,1792]{3,2,1,0:T(8,128)(2,1)S(1)}, bf16[2,4,64,1792]{3,2,1,0:T(8,128)(2,1)}, u32[]{:S(2)}) %copy-start) | copy-done | bytes 1835032
  131.0 0.0 copy-start.1
  131.0 1.5 %copy-done.1 = bf16[2,4,64,1792]{3,2,1,0:T(8,128)(2,1)S(1)} copy-done((bf16[2,4,64,1792]{3,2,1,0:T(8,128)(2,1)S(1)}, bf16[2,4,64,1792]{3,2,1,0:T(8,128)(2,1)}, u32[]{:S(2)}) %copy-start.1) | copy-done | bytes 1835032
  132.5 0.0 copy-start.2
  132.5 1.6 %copy-done.2 = bf16[2,2048,256]{2,1,0:T(8,128)(2,1)S(1)} copy-done((bf16[2,2048,256]{2,1,0:T(8,128)(2,1)S(1)}, bf16[2,2048,256]{2,1,0:T(8,128)(2,1)}, u32[]{:S(2)}) %copy-start.2) | copy-done | bytes 2097176
  134.1 0.0 copy-start.3
  134.1 10.1 %shard_map.76 = (bf16[2048,1792]{1,0:T(8,128)(2,1)}, bf16[2048,1792]{1,0:T(8,128)(2,1)}) custom-call(bf16[2,2048,256]{2,1,0:T(8,128)(2,1)S(1)} %copy-done.2, bf16[2,256,1792]{2,1,0:T(8,128)(2,1)S(1)} %bitcast.2, bf16[2,256,1792]{2,1,0:T(8,128)(2,1)S(1)} %bitcast.3), custom_call_target="tpu_custom_call" | custom-call | flops 7516192768 | bytes 18350080 | tf_op jit(solution)/shard_map/pallas_call | solution.py:468
  144.2 0.0 collective-permute-done
  144.2 0.0 collective-permute-done.2
  144.2 0.0 collective-permute-done.1
  144.3 1.8 %add_convert_fusion = bf16[64,2048]{1,0:T(8,128)(2,1)} fusion(bf16[64,2048]{1,0:T(8,128)(2,1)S(1)} %collective-permute-done.2, bf16[64,2048]{1,0:T(8,128)(2,1)S(1)} %collective-permute-done.1, bf16[64,2048]{1,0:T(8,128)(2,1)S(1)} %collective-permute-done, bf16[256,2048]{1,0:T(8,128)(2,1)} %get-tuple-element.12, s32[]{:T(128)S(6)} %select_n.12), kind=kLoop, calls=%fused_computation | loop fusion | flops 1048576 | bytes 1310724 | tf_op jit(solution)/shard_map/convert_element_type | solution.py:494
  146.0 0.0 copy-done.3
  146.0 0.8 copy.9
Async XLA Ops:
  125.9 18.3 %collective-permute-start = (bf16[64,2048]{1,0:T(8,128)(2,1)S(1)}, bf16[64,2048]{1,0:T(8,128)(2,1)S(1)}, u32[]{:S(2)}, u32[]{:S(2)}) collective-permute-start(bf16[64,2048]{1,0:T(8,128)(2,1)S(1)} %get-tuple-element.18), channel_id=1, source_target_pairs={{0,2},{2,4},{4,6},{6,0},{1,3},{3,5},{5,7},{7,1},{8,10},{10,12},{12... | collective-permute-start | bytes 786440 | tf_op jit(solution)/shard_map/ppermute | solution.py:493
  126.0 18.3 %collective-permute-start.2 = (bf16[64,2048]{1,0:T(8,128)(2,1)S(1)}, bf16[64,2048]{1,0:T(8,128)(2,1)S(1)}, u32[]{:S(2)}, u32[]{:S(2)}) collective-permute-start(bf16[64,2048]{1,0:T(8,128)(2,1)S(1)} %get-tuple-element.19), channel_id=1, source_target_pairs={{0,6},{2,0},{4,2},{6,4},{1,7},{3,1},{5,3},{7,5},{8,14},{10,8},{12,... | collective-permute-start | bytes 786440 | tf_op jit(solution)/shard_map/ppermute | solution.py:493
  127.7 16.5 %collective-permute-start.1 = (bf16[64,2048]{1,0:T(8,128)(2,1)S(1)}, bf16[64,2048]{1,0:T(8,128)(2,1)S(1)}, u32[]{:S(2)}, u32[]{:S(2)}) collective-permute-start(bf16[64,2048]{1,0:T(8,128)(2,1)S(1)} %get-tuple-element.20), channel_id=1, source_target_pairs={{0,4},{2,6},{4,0},{6,2},{1,5},{3,7},{5,1},{7,3},{8,12},{10,14},{12... | collective-permute-start | bytes 786440 | tf_op jit(solution)/shard_map/ppermute | solution.py:493
  129.5 1.5 %copy-start = (bf16[2,4,64,1792]{3,2,1,0:T(8,128)(2,1)S(1)}, bf16[2,4,64,1792]{3,2,1,0:T(8,128)(2,1)}, u32[]{:S(2)}) copy-start(bf16[2,4,64,1792]{3,2,1,0:T(8,128)(2,1)} %get-tuple-element.14) | copy-start | bytes 5505028
  131.0 1.5 %copy-start.1 = (bf16[2,4,64,1792]{3,2,1,0:T(8,128)(2,1)S(1)}, bf16[2,4,64,1792]{3,2,1,0:T(8,128)(2,1)}, u32[]{:S(2)}) copy-start(bf16[2,4,64,1792]{3,2,1,0:T(8,128)(2,1)} %get-tuple-element.15) | copy-start | bytes 5505028
  132.5 1.6 %copy-start.2 = (bf16[2,2048,256]{2,1,0:T(8,128)(2,1)S(1)}, bf16[2,2048,256]{2,1,0:T(8,128)(2,1)}, u32[]{:S(2)}) copy-start(bf16[2,2048,256]{2,1,0:T(8,128)(2,1)} %get-tuple-element.13.tokens_ref) | copy-start | bytes 6291460
  134.1 11.9 %copy-start.3 = (bf16[64,3584]{1,0:T(8,128)(2,1)S(1)}, bf16[64,3584]{1,0:T(8,128)(2,1)}, u32[]{:S(2)}) copy-start(bf16[64,3584]{1,0:T(8,128)(2,1)} %get-tuple-element.25) | copy-start | bytes 1376260

commit v6 on v5

--- a/solution.py
+++ b/solution.py
@@ -471,7 +471,7 @@
         in_specs=[pl.BlockSpec((n_dep, depth, tokens_n), lambda i: (0, 0, 0)), taken, taken],
         out_specs=(given, given),
         out_shape=(shape, shape),
-        compiler_params=pltpu.CompilerParams(vmem_limit_bytes=48 * 1024 * 1024),
+        compiler_params=pltpu.CompilerParams(vmem_limit_bytes=60 * 1024 * 1024),
         cost_estimate=pl.CostEstimate(
             flops=4 * n_dep * tokens_n * depth * share,
             bytes_accessed=4 * depth * share + 4 * n_dep * tokens_n * share,

time: 147 us -> 145 us (0.986)
  local copies, waits for them, and re-layouts: 6.53 us -> 1.94 us
  Pallas kernels: 134 us -> 136 us
    unnamed x9 -> x3, local copies, waits for them, and re-layouts: 5.36 us -> 0.77 us
    pallas_call x1, Pallas kernels: 10.1 us -> 12.1 us  [weight_grads(): pl.pallas_call(weight_grad_kernel, grid=(share // wide,), in_specs=[pl.Bl...]
  transfers between devices with their start and end apart: 3 -> 3, of which waited for: 0 -> 0; matrix products, arithmetic and copies ran while one was open for 0% -> 0% of each run, Pallas kernels for 7% -> 8%
where the time goes in v6:
time: 145 us; the launch traced here: 144 us
  Pallas kernels  136 us (94%)
  starting transfers between devices  3.6 us (2%)
  local copies, waits for them, and re-layouts  1.94 us (1%)
  other arithmetic  1.79 us (1%)
    pallas_call x1, Pallas kernels, exchange(): pl.pallas_call(functools.partial(kernel, n_row, n_col, n_dep, w), out_sha...  124 us
    pallas_call x1, Pallas kernels, weight_grads(): pl.pallas_call(weight_grad_kernel, grid=(share // wide,), in_specs=[pl.Bl...  12.1 us
    ppermute x3, starting transfers between devices, on_device(): lax.ppermute(block, 'col', [(i, (i + step) % n_col) for i in range(n_col)])  3.6 us
  transfers between devices with their start and end apart: 3, of which 0 were waited for; matrix products, arithmetic and copies ran while one was open for 0% of the time, Pallas kernels for 8%

profile of v6, /device:TPU:0, one launch (start us, length us, event | category | flops | bytes accessed | tf_op | source)
XLA Modules:
  0.0 144.2 jit_solution(5136107590806354723)
XLA Ops:
  0.7 124.1 %shard_map.75 = (bf16[64,3584]{1,0:T(8,128)(2,1)}, bf16[256,2048]{1,0:T(8,128)(2,1)}, bf16[2,2048,256]{2,1,0:T(8,128)(2,1)}, bf16[2,4,64,1792]{3,2,1,0:T(8,128)(2,1)}, bf16[2,4,64,1792]{3,2,1,0:T(8,128)(2,1)}) custom-call(bf16[64,2048]{1,0:T(8,128)(2,1)} %tokens_ref.1, bf16[2048,3584]{1,0:T(8,128)(2,1)} %gate_w_ref.1, bf16[2048,3584]{1,0:T(8,128)(2,1)} %up_w_ref.1, ...), custom_call_target="tpu_custom_call" | custom-call | flops 15032385536 | bytes 29360128 | tf_op jit(solution)/shard_map/pallas_call | solution.py:409
  124.7 1.2 constant_dynamic-slice_fusion.2
  125.9 0.1 collective-permute-start
  126.0 1.7 %collective-permute-start.2 = (bf16[64,2048]{1,0:T(8,128)(2,1)S(1)}, bf16[64,2048]{1,0:T(8,128)(2,1)S(1)}, u32[]{:S(2)}, u32[]{:S(2)}) collective-permute-start(bf16[64,2048]{1,0:T(8,128)(2,1)S(1)} %get-tuple-element.19), channel_id=1, source_target_pairs={{0,6},{2,0},{4,2},{6,4},{1,7},{3,1},{5,3},{7,5},{8,14},{10,8},{12,... | collective-permute-start | bytes 786440 | tf_op jit(solution)/shard_map/ppermute | solution.py:493
  127.7 1.8 %collective-permute-start.1 = (bf16[64,2048]{1,0:T(8,128)(2,1)S(1)}, bf16[64,2048]{1,0:T(8,128)(2,1)S(1)}, u32[]{:S(2)}, u32[]{:S(2)}) collective-permute-start(bf16[64,2048]{1,0:T(8,128)(2,1)S(1)} %get-tuple-element.20), channel_id=1, source_target_pairs={{0,4},{2,6},{4,0},{6,2},{1,5},{3,7},{5,1},{7,3},{8,12},{10,14},{12... | collective-permute-start | bytes 786440 | tf_op jit(solution)/shard_map/ppermute | solution.py:493
  129.5 0.0 copy-start
  129.5 12.1 %shard_map.76 = (bf16[2048,1792]{1,0:T(8,128)(2,1)}, bf16[2048,1792]{1,0:T(8,128)(2,1)}) custom-call(bf16[2,2048,256]{2,1,0:T(8,128)(2,1)} %get-tuple-element.13.tokens_ref, bf16[2,256,1792]{2,1,0:T(8,128)(2,1)} %bitcast.2, bf16[2,256,1792]{2,1,0:T(8,128)(2,1)} %bitcast.3), custom_call_target="tpu_custom_call" | custom-call | flops 7516192768 | bytes 18350080 | tf_op jit(solution)/shard_map/pallas_call | solution.py:468
  141.6 0.0 collective-permute-done
  141.6 0.0 collective-permute-done.2
  141.6 0.0 collective-permute-done.1
  141.6 1.8 %add_convert_fusion = bf16[64,2048]{1,0:T(8,128)(2,1)} fusion(bf16[64,2048]{1,0:T(8,128)(2,1)S(1)} %collective-permute-done.2, bf16[64,2048]{1,0:T(8,128)(2,1)S(1)} %collective-permute-done.1, bf16[64,2048]{1,0:T(8,128)(2,1)S(1)} %collective-permute-done, bf16[256,2048]{1,0:T(8,128)(2,1)} %get-tuple-element.12, s32[]{:T(128)S(6)} %select_n.12), kind=kLoop, calls=%fused_computation | loop fusion | flops 1048576 | bytes 1310724 | tf_op jit(solution)/shard_map/convert_element_type | solution.py:494
  143.4 0.0 copy-done
  143.4 0.8 copy.9
Async XLA Ops:
  125.9 15.7 %collective-permute-start = (bf16[64,2048]{1,0:T(8,128)(2,1)S(1)}, bf16[64,2048]{1,0:T(8,128)(2,1)S(1)}, u32[]{:S(2)}, u32[]{:S(2)}) collective-permute-start(bf16[64,2048]{1,0:T(8,128)(2,1)S(1)} %get-tuple-element.18), channel_id=1, source_target_pairs={{0,2},{2,4},{4,6},{6,0},{1,3},{3,5},{5,7},{7,1},{8,10},{10,12},{12... | collective-permute-start | bytes 786440 | tf_op jit(solution)/shard_map/ppermute | solution.py:493
  126.0 15.6 %collective-permute-start.2 = (bf16[64,2048]{1,0:T(8,128)(2,1)S(1)}, bf16[64,2048]{1,0:T(8,128)(2,1)S(1)}, u32[]{:S(2)}, u32[]{:S(2)}) collective-permute-start(bf16[64,2048]{1,0:T(8,128)(2,1)S(1)} %get-tuple-element.19), channel_id=1, source_target_pairs={{0,6},{2,0},{4,2},{6,4},{1,7},{3,1},{5,3},{7,5},{8,14},{10,8},{12,... | collective-permute-start | bytes 786440 | tf_op jit(solution)/shard_map/ppermute | solution.py:493
  127.7 13.9 %collective-permute-start.1 = (bf16[64,2048]{1,0:T(8,128)(2,1)S(1)}, bf16[64,2048]{1,0:T(8,128)(2,1)S(1)}, u32[]{:S(2)}, u32[]{:S(2)}) collective-permute-start(bf16[64,2048]{1,0:T(8,128)(2,1)S(1)} %get-tuple-element.20), channel_id=1, source_target_pairs={{0,4},{2,6},{4,0},{6,2},{1,5},{3,7},{5,1},{7,3},{8,12},{10,14},{12... | collective-permute-start | bytes 786440 | tf_op jit(solution)/shard_map/ppermute | solution.py:493
  129.5 13.9 %copy-start = (bf16[64,3584]{1,0:T(8,128)(2,1)S(1)}, bf16[64,3584]{1,0:T(8,128)(2,1)}, u32[]{:S(2)}) copy-start(bf16[64,3584]{1,0:T(8,128)(2,1)} %get-tuple-element.25) | copy-start | bytes 1376260
